TPU v7x, 256 devices: a whole 4x4x8 slice. The times are simulated.
256 devices in a mesh: shot: 16 (over y, x), space: 16 (over z, core).
Axes of the slice: x: 4, y: 4, z: 8, core: 2. Of those that a mesh axis runs over, the one named last changes fastest.
Arguments:
- right_side: float32 [2, 256, 16, 16, 16, 128], P(None, 'shot', 'space'), may hold values from -6 to 6
- wavenumber_sq: float32 [16, 16, 16, 128], P('space'), may hold values from 0.2 to 1.2
- source_cell: int32 [256], P('shot'), may hold values from 0 to 524287
- source_amplitude: float32 [2, 256], P(None, 'shot'), may hold values from -16 to 16
Outputs:
- wavefield: float32 [2, 256, 16, 16, 16, 128], P(None, 'shot', 'space')
All inputs are finite; a program needn't handle non-finite values.
Results may differ from a plain program's by a relative error of at most 0.0003.
Values sent between devices are 32-bit elements; how exact they have to be, the bound alone decides.
No kernel may reach another device: no remote copies, remote signals or barrier semaphores. Data moves between devices by JAX's collectives and lax.ppermute only.
A program may use at most 128 MiB of HBM per device.

v0:
```python
import jax
import jax.numpy as jnp
from jax import lax
from jax.sharding import PartitionSpec as P

TY = 4
COARSE = 4


OMEGA = 0.8
BETA = 0.5


def passed_along(value, axis, steps):
    count = lax.axis_size(axis)
    leading, last = (max(0, -steps), min(count, count - steps))
    return lax.ppermute(value, axis, [(source, source + steps) for source in range(leading, last)])


def inverse_diag(diag_r, diag_i):
    scale = 1.0 / (diag_r * diag_r + diag_i * diag_i)
    return (diag_r * scale, -diag_i * scale)


def coarsen(field):
    lead = field.shape[:-3]
    width_x, width_y, depth = field.shape[-3:]
    shaped = field.reshape(lead + (width_x // 2, 2, width_y // 2, 2, depth))
    total = shaped[..., :, 0, :, 0, :] + shaped[..., :, 1, :, 0, :]
    total = total + shaped[..., :, 0, :, 1, :] + shaped[..., :, 1, :, 1, :]
    return 0.25 * total


def refine(field):
    return jnp.repeat(jnp.repeat(field, 2, axis=-3), 2, axis=-2)


def relax(field, rhs, image, inv_r, inv_i):
    rest_r = rhs[0] - image[0]
    rest_i = rhs[1] - image[1]
    real = field[0] + OMEGA * (inv_r * rest_r - inv_i * rest_i)
    imag = field[1] + OMEGA * (inv_r * rest_i + inv_i * rest_r)
    return jnp.stack([real, imag])


def tile_operator(field, faces, diag_r, diag_i, weight_x):
    low_x, high_x, low_y, high_y = faces
    wide_x = jnp.concatenate([low_x, field, high_x], axis=2)
    wide_y = jnp.concatenate([low_y, field, high_y], axis=3)
    flat = jnp.zeros_like(field[..., :1])
    wide_z = jnp.concatenate([flat, field, flat], axis=4)
    along_x = wide_x[:, :, 2:] + wide_x[:, :, :-2]
    along_y = wide_y[:, :, :, 2:] + wide_y[:, :, :, :-2]
    along_z = wide_z[..., 2:] + wide_z[..., :-2]
    near = weight_x * (along_x + along_y) + along_z
    real = diag_r * field[0] - diag_i * field[1] - near[0]
    imag = diag_r * field[1] + diag_i * field[0] - near[1]
    return jnp.stack([real, imag])


def fine_faces(field):
    received = []
    for offset, face in ((TY, field[:, :, -1:]), (-TY, field[:, :, :1])):
        received.append(passed_along(face, "space", offset))
    column = lax.axis_index("space") % TY
    for offset, face, keep in (
        (1, field[:, :, :, -1:], column > 0),
        (-1, field[:, :, :, :1], column < TY - 1),
    ):
        received.append(jnp.where(keep, passed_along(face, "space", offset), 0.0))
    return received


def coarse_faces(field):
    received = []
    for offset, face in ((TY, field[:, :, -1:]), (-TY, field[:, :, :1])):
        received.append(passed_along(face, "space", offset))
    column = lax.axis_index("space") % TY
    for offset, face, keep in (
        (1, field[:, :, :, -1:], column > 0),
        (-1, field[:, :, :, :1], column < TY - 1),
    ):
        received.append(jnp.where(keep, passed_along(face, "space", offset), 0.0))
    return received


def shards(right_side, wavenumber_sq, source_cell, source_amplitude):
    rhs = right_side[:, :, 0]
    k_fine = wavenumber_sq[0]
    shots, block, depth = (rhs.shape[1], rhs.shape[2], rhs.shape[4])
    tile = lax.axis_index("space")
    row = tile // TY
    column = tile % TY
    width_y = block * TY
    grid_x = source_cell // (width_y * depth)
    grid_y = source_cell // depth % width_y
    grid_z = source_cell % depth
    local = jnp.arange(block, dtype=jnp.int32)
    hit_x = (row * block + local[None, :] == grid_x[:, None]).astype(jnp.float32)
    hit_y = (column * block + local[None, :] == grid_y[:, None]).astype(jnp.float32)
    hit_z = (jnp.arange(depth, dtype=jnp.int32)[None, :] == grid_z[:, None]).astype(jnp.float32)
    hit = hit_x[:, :, None, None] * hit_y[:, None, :, None] * hit_z[:, None, None, :]
    rhs = rhs + source_amplitude[:, :, None, None, None] * hit[None]
    fine_r = 6.0 - k_fine
    fine_i = BETA * k_fine
    inv_r, inv_i = inverse_diag(fine_r, fine_i)
    empty = jnp.zeros_like(rhs)
    field = relax(empty, rhs, empty, inv_r, inv_i)
    image = tile_operator(field, fine_faces(field), fine_r, fine_i, 1.0)
    field = relax(field, rhs, image, inv_r, inv_i)
    rest = rhs - tile_operator(field, fine_faces(field), fine_r, fine_i, 1.0)
    coarse_rhs = coarsen(rest)
    k_coarse = coarsen(k_fine)
    coarse_r = 3.0 - k_coarse
    coarse_i = BETA * k_coarse
    cinv_r, cinv_i = inverse_diag(coarse_r, coarse_i)
    blank = jnp.zeros_like(coarse_rhs)
    corr = relax(blank, coarse_rhs, blank, cinv_r, cinv_i)
    for sweep in range(COARSE - 1):
        image_c = tile_operator(corr, coarse_faces(corr), coarse_r, coarse_i, 0.25)
        corr = relax(corr, coarse_rhs, image_c, cinv_r, cinv_i)
    field = field + refine(corr)
    image = tile_operator(field, fine_faces(field), fine_r, fine_i, 1.0)
    field = relax(field, rhs, image, inv_r, inv_i)
    return field[:, :, None]


def solution(mesh):
    return jax.shard_map(
        shards,
        mesh=mesh,
        in_specs=(
            P(None, "shot", "space", None, None, None),
            P("space", None, None, None),
            P("shot"),
            P(None, "shot"),
        ),
        out_specs=P(None, "shot", "space", None, None, None),
        check_vma=False,
    )
```

profile of v0, /device:TPU:69, one launch (start us, length us, event | category | flops | bytes accessed | tf_op | source)
XLA Modules:
  0.0 182.2 jit_solution(835124737062812967)
XLA Ops:
  2.5 3.0 %bitcast_add_fusion = f32[2,16,16,16,128]{4,3,2,1,0:T(8,128)S(1)} fusion(f32[2,16,1,16,16,128]{5,4,3,2,1,0:T(8,128)} %param.4, f32[16,16,16,128]{3,2,1,0:T(8,128)S(1)} %broadcast_multiply_fusion.3, f32[2,16]{1,0:T(2,128)S(1)} %copy-done.10), kind=kLoop, calls=%fused_computation.61 | loop fusion | flops 2097152 | bytes 10485888 | tf_op jit(solution)/shard_map/add | solution.py:103
  5.5 3.3 %broadcast_multiply_fusion.1 = (f32[1,16,16,16,128]{4,3,2,1,0:T(8,128)S(1)}, f32[1,16,16,16,128]{4,3,2,1,0:T(8,128)}, f32[1,16,16,16,128]{4,3,2,1,0:T(8,128)S(1)}, f32[1,16,16,16,128]{4,3,2,1,0:T(8,128)}) fusion(f32[2,16,16,16,128]{4,3,2,1,0:T(8,128)S(1)} %bitcast_add_fusion, f32[16,16,128]{2,1,0:T(8,128)S(1)} %get-tuple-element.59, ...), kind=kLoop, calls=%fused_computation.159 | loop fusion | flops 4194304 | bytes 12845056 | tf_op jit(solution)/shard_map/mul | solution.py:42
  11.6 6.2 %collective-permute-start.1 = (f32[2,16,1,16,128]{4,3,2,1,0:T(8,128)S(1)}, f32[2,16,1,16,128]{4,3,2,1,0:T(8,128)}, u32[]{:S(2)}, u32[]{:S(2)}) collective-permute-start(f32[2,16,1,16,128]{4,3,2,1,0:T(8,128)S(1)} %get-tuple-element.37), channel_id=1, source_target_pairs={{0,4},{1,5},{2,6},{3,7},{4,8},{5,9},{6,10},{7,11},{8,12},{9,13},{1... | collective-permute-start | bytes 786440 | tf_op jit(solution)/shard_map/ppermute | solution.py:17
  22.0 3.1 %collective-permute-start.3 = (f32[2,16,16,1,128]{4,3,2,1,0:T(1,128)}, f32[2,16,16,1,128]{4,3,2,1,0:T(1,128)}, u32[]{:S(2)}, u32[]{:S(2)}) collective-permute-start(f32[2,16,16,1,128]{4,3,2,1,0:T(1,128)} %get-tuple-element.39), channel_id=1, source_target_pairs={{0,1},{1,2},{2,3},{3,4},{4,5},{5,6},{6,7},{7,8},{8,9},{9,10},{10,1... | collective-permute-start | bytes 786440 | tf_op jit(solution)/shard_map/ppermute | solution.py:17
  25.7 3.4 %broadcast_multiply_fusion = f32[16,8,2,8,2,128]{5,4,3,2,1,0:T(2,128)} fusion(f32[16,128]{1,0:T(8,128)S(1)} %fusion.65, f32[16,8,2,8,2]{4,3,2,1,0:T(8,128)S(1)} %broadcast_multiply_fusion.4), kind=kLoop, calls=%fused_computation.158 | loop fusion | flops 524288 | bytes 2121728 | tf_op jit(solution)/shard_map/mul | solution.py:102
  34.2 11.6 %fusion.1 = f32[2,16,16,16,128]{4,3,2,1,0:T(8,128)S(1)} fusion(f32[2,16,16,16,128]{4,3,2,1,0:T(8,128)} %pad_maximum_fusion, f32[2,16,16,1,128]{4,3,2,1,0:T(1,128)S(1)} %broadcast_select_fusion.2, f32[1,16,16,16,128]{4,3,2,1,0:T(8,128)} %copy-done.2, f32[1,16,16,16,128]{4,3,2,1,0:T(8,128)} %copy-done.3, f32[2,16,16,1,128]{4,3,2,1,0:T(1,128)S(1)} %broadcast_select_fusion.5, ...), kind=kLoop, calls=%fused_computation.25 | loop fusion | flops 13631488 | bytes 13631488 | tf_op jit(solution)/shard_map/add | solution.py:55
  50.8 3.9 %collective-permute-start.7 = (f32[2,16,16,1,128]{4,3,2,1,0:T(1,128)S(1)}, f32[2,16,16,1,128]{4,3,2,1,0:T(1,128)S(1)}, u32[]{:S(2)}, u32[]{:S(2)}) collective-permute-start(f32[2,16,16,1,128]{4,3,2,1,0:T(1,128)S(1)} %get-tuple-element.35), channel_id=1, source_target_pairs={{0,1},{1,2},{2,3},{3,4},{4,5},{5,6},{6,7},{7,8},{8,9},{9,10},{10,1... | collective-permute-start | bytes 786440 | tf_op jit(solution)/shard_map/ppermute | solution.py:17
  57.1 5.7 %collective-permute-start.5 = (f32[2,16,1,16,128]{4,3,2,1,0:T(8,128)S(1)}, f32[2,16,1,16,128]{4,3,2,1,0:T(8,128)S(1)}, u32[]{:S(2)}, u32[]{:S(2)}) collective-permute-start(f32[2,16,1,16,128]{4,3,2,1,0:T(8,128)S(1)} %get-tuple-element.33), channel_id=1, source_target_pairs={{0,4},{1,5},{2,6},{3,7},{4,8},{5,9},{6,10},{7,11},{8,12},{9,13},{1... | collective-permute-start | bytes 786440 | tf_op jit(solution)/shard_map/ppermute | solution.py:17
  63.3 8.5 %collective-permute-done.4 = f32[2,16,1,16,128]{4,3,2,1,0:T(8,128)S(1)} collective-permute-done((f32[2,16,1,16,128]{4,3,2,1,0:T(8,128)S(1)}, f32[2,16,1,16,128]{4,3,2,1,0:T(8,128)S(1)}, u32[]{:S(2)}, u32[]{:S(2)}) %collective-permute-start.4) | collective-permute-done | bytes 262176 | tf_op jit(solution)/shard_map/ppermute | solution.py:17
  73.6 2.9 %fusion.3 = f32[2,16,16,16,128]{4,3,2,1,0:T(8,128)S(1)} fusion(f32[2,16,16,16,128]{4,3,2,1,0:T(8,128)S(1)} %pad_maximum_fusion.1, f32[2,16,16,1,128]{4,3,2,1,0:T(1,128)S(1)} %broadcast_select_fusion.1, f32[1,16,16,16,128]{4,3,2,1,0:T(8,128)S(1)} %multiply_add_fusion.2, f32[1,16,16,16,128]{4,3,2,1,0:T(8,128)S(1)} %get-tuple-element.17, ...), kind=kLoop, calls=%fused_computation.27 | loop fusion | flops 13631488 | bytes 13631488 | tf_op jit(solution)/shard_map/add | solution.py:55
  79.4 5.1 %maximum_subtract_fusion = f32[2,16,8,2,8,2,128]{6,5,4,3,2,1,0:T(2,128)S(1)} fusion(f32[1,16,8,2,8,2,128]{6,5,4,3,2,1,0:T(2,128)S(1)} %bitcast.70, f32[1,16,8,2,8,2,128]{6,5,4,3,2,1,0:T(2,128)S(1)} %bitcast.69, f32[2,16,8,2,8,2,128]{6,5,4,3,2,1,0:T(2,128)S(1)} %bitcast.59, f32[16,8,2,8,2,128]{5,4,3,2,1,0:T(2,128)S(1)} %copy-done.8, f32[2,16]{1,0:T(2,128)S(1)} %copy-done.10), kind=kLoop, calls=%fused_computation.59 | loop fusion | flops 4194304 | bytes 14680192 | tf_op jit(solution)/shard_map/sub | solution.py:111
  89.3 6.0 %collective-permute-start.9 = (f32[2,16,1,8,128]{4,3,2,1,0:T(8,128)S(1)}, f32[2,16,1,8,128]{4,3,2,1,0:T(8,128)S(1)}, u32[]{:S(2)}, u32[]{:S(2)}) collective-permute-start(f32[2,16,1,8,128]{4,3,2,1,0:T(8,128)S(1)} %get-tuple-element.55), channel_id=1, source_target_pairs={{0,4},{1,5},{2,6},{3,7},{4,8},{5,9},{6,10},{7,11},{8,12},{9,13},{1... | collective-permute-start | bytes 393224 | tf_op jit(solution)/shard_map/ppermute | solution.py:17
  97.5 3.4 %collective-permute-start.11 = (f32[2,16,8,1,128]{4,3,2,1,0:T(1,128)S(1)}, f32[2,16,8,1,128]{4,3,2,1,0:T(1,128)S(1)}, u32[]{:S(2)}, u32[]{:S(2)}) collective-permute-start(f32[2,16,8,1,128]{4,3,2,1,0:T(1,128)S(1)} %get-tuple-element.57), channel_id=1, source_target_pairs={{0,1},{1,2},{2,3},{3,4},{4,5},{5,6},{6,7},{7,8},{8,9},{9,10},{10,1... | collective-permute-start | bytes 393224 | tf_op jit(solution)/shard_map/ppermute | solution.py:17
  106.3 5.5 %collective-permute-start.13 = (f32[2,16,1,8,128]{4,3,2,1,0:T(8,128)S(1)}, f32[2,16,1,8,128]{4,3,2,1,0:T(8,128)S(1)}, u32[]{:S(2)}, u32[]{:S(2)}) collective-permute-start(f32[2,16,1,8,128]{4,3,2,1,0:T(8,128)S(1)} %get-tuple-element.51), channel_id=1, source_target_pairs={{0,4},{1,5},{2,6},{3,7},{4,8},{5,9},{6,10},{7,11},{8,12},{9,13},{1... | collective-permute-start | bytes 393224 | tf_op jit(solution)/shard_map/ppermute | solution.py:17
  111.8 3.5 %collective-permute-start.14 = (f32[2,16,8,1,128]{4,3,2,1,0:T(1,128)S(1)}, f32[2,16,8,1,128]{4,3,2,1,0:T(1,128)S(1)}, u32[]{:S(2)}, u32[]{:S(2)}) collective-permute-start(f32[2,16,8,1,128]{4,3,2,1,0:T(1,128)S(1)} %get-tuple-element.52), channel_id=1, source_target_pairs={{1,0},{2,1},{3,2},{4,3},{5,4},{6,5},{7,6},{8,7},{9,8},{10,9},{11,1... | collective-permute-start | bytes 393224 | tf_op jit(solution)/shard_map/ppermute | solution.py:17
  115.2 3.4 %collective-permute-start.15 = (f32[2,16,8,1,128]{4,3,2,1,0:T(1,128)S(1)}, f32[2,16,8,1,128]{4,3,2,1,0:T(1,128)S(1)}, u32[]{:S(2)}, u32[]{:S(2)}) collective-permute-start(f32[2,16,8,1,128]{4,3,2,1,0:T(1,128)S(1)} %get-tuple-element.53), channel_id=1, source_target_pairs={{0,1},{1,2},{2,3},{3,4},{4,5},{5,6},{6,7},{7,8},{8,9},{9,10},{10,1... | collective-permute-start | bytes 393224 | tf_op jit(solution)/shard_map/ppermute | solution.py:17
  123.9 5.5 %collective-permute-start.17 = (f32[2,16,1,8,128]{4,3,2,1,0:T(8,128)S(1)}, f32[2,16,1,8,128]{4,3,2,1,0:T(8,128)S(1)}, u32[]{:S(2)}, u32[]{:S(2)}) collective-permute-start(f32[2,16,1,8,128]{4,3,2,1,0:T(8,128)S(1)} %get-tuple-element.47), channel_id=1, source_target_pairs={{0,4},{1,5},{2,6},{3,7},{4,8},{5,9},{6,10},{7,11},{8,12},{9,13},{1... | collective-permute-start | bytes 393224 | tf_op jit(solution)/shard_map/ppermute | solution.py:17
  129.4 3.5 %collective-permute-start.18 = (f32[2,16,8,1,128]{4,3,2,1,0:T(1,128)S(1)}, f32[2,16,8,1,128]{4,3,2,1,0:T(1,128)S(1)}, u32[]{:S(2)}, u32[]{:S(2)}) collective-permute-start(f32[2,16,8,1,128]{4,3,2,1,0:T(1,128)S(1)} %get-tuple-element.48), channel_id=1, source_target_pairs={{1,0},{2,1},{3,2},{4,3},{5,4},{6,5},{7,6},{8,7},{9,8},{10,9},{11,1... | collective-permute-start | bytes 393224 | tf_op jit(solution)/shard_map/ppermute | solution.py:17
  132.9 3.6 %collective-permute-start.19 = (f32[2,16,8,1,128]{4,3,2,1,0:T(1,128)S(1)}, f32[2,16,8,1,128]{4,3,2,1,0:T(1,128)S(1)}, u32[]{:S(2)}, u32[]{:S(2)}) collective-permute-start(f32[2,16,8,1,128]{4,3,2,1,0:T(1,128)S(1)} %get-tuple-element.49), channel_id=1, source_target_pairs={{0,1},{1,2},{2,3},{3,4},{4,5},{5,6},{6,7},{7,8},{8,9},{9,10},{10,1... | collective-permute-start | bytes 393224 | tf_op jit(solution)/shard_map/ppermute | solution.py:17
  141.1 5.1 %broadcast_in_dim.26 = f32[2,16,16,8,2,128]{5,4,3,2,1,0:T(2,128)} broadcast(f32[2,16,16,8,128]{4,3,2,1,0:T(8,128)} %bitcast.68), dimensions={0,1,2,3,5} | broadcast | bytes 6291456 | tf_op jit(solution)/shard_map/broadcast_in_dim | solution.py:35
  149.3 2.9 %collective-permute-start.22 = (f32[2,16,16,1,128]{4,3,2,1,0:T(1,128)S(1)}, f32[2,16,16,1,128]{4,3,2,1,0:T(1,128)S(1)}, u32[]{:S(2)}, u32[]{:S(2)}) collective-permute-start(f32[2,16,16,1,128]{4,3,2,1,0:T(1,128)S(1)} %get-tuple-element.30), channel_id=1, source_target_pairs={{1,0},{2,1},{3,2},{4,3},{5,4},{6,5},{7,6},{8,7},{9,8},{10,9},{11,1... | collective-permute-start | bytes 786440 | tf_op jit(solution)/shard_map/ppermute | solution.py:17
  152.3 3.4 %collective-permute-start.23 = (f32[2,16,16,1,128]{4,3,2,1,0:T(1,128)S(1)}, f32[2,16,16,1,128]{4,3,2,1,0:T(1,128)S(1)}, u32[]{:S(2)}, u32[]{:S(2)}) collective-permute-start(f32[2,16,16,1,128]{4,3,2,1,0:T(1,128)S(1)} %get-tuple-element.31), channel_id=1, source_target_pairs={{0,1},{1,2},{2,3},{3,4},{4,5},{5,6},{6,7},{7,8},{8,9},{9,10},{10,1... | collective-permute-start | bytes 786440 | tf_op jit(solution)/shard_map/ppermute | solution.py:17
  157.6 5.5 %collective-permute-start.21 = (f32[2,16,1,16,128]{4,3,2,1,0:T(8,128)S(1)}, f32[2,16,1,16,128]{4,3,2,1,0:T(8,128)S(1)}, u32[]{:S(2)}, u32[]{:S(2)}) collective-permute-start(f32[2,16,1,16,128]{4,3,2,1,0:T(8,128)S(1)} %get-tuple-element.29), channel_id=1, source_target_pairs={{0,4},{1,5},{2,6},{3,7},{4,8},{5,9},{6,10},{7,11},{8,12},{9,13},{1... | collective-permute-start | bytes 786440 | tf_op jit(solution)/shard_map/ppermute | solution.py:17
  163.6 8.6 %collective-permute-done.20 = f32[2,16,1,16,128]{4,3,2,1,0:T(8,128)S(1)} collective-permute-done((f32[2,16,1,16,128]{4,3,2,1,0:T(8,128)S(1)}, f32[2,16,1,16,128]{4,3,2,1,0:T(8,128)S(1)}, u32[]{:S(2)}, u32[]{:S(2)}) %collective-permute-start.20) | collective-permute-done | bytes 262176 | tf_op jit(solution)/shard_map/ppermute | solution.py:17
  (119 shorter events, 65.0 us)
Async XLA Ops:
  9.7 24.5 %collective-permute-start = (f32[2,16,1,16,128]{4,3,2,1,0:T(8,128)}, f32[2,16,1,16,128]{4,3,2,1,0:T(8,128)}, u32[]{:S(2)}, u32[]{:S(2)}) collective-permute-start(f32[2,16,1,16,128]{4,3,2,1,0:T(8,128)} %get-tuple-element.36), channel_id=1, source_target_pairs={{4,0},{5,1},{6,2},{7,3},{8,4},{9,5},{10,6},{11,7},{12,8},{13,9},{1... | collective-permute-start | bytes 786440 | tf_op jit(solution)/shard_map/ppermute | solution.py:17
  11.6 22.6 %collective-permute-start.1 = (f32[2,16,1,16,128]{4,3,2,1,0:T(8,128)S(1)}, f32[2,16,1,16,128]{4,3,2,1,0:T(8,128)}, u32[]{:S(2)}, u32[]{:S(2)}) collective-permute-start(f32[2,16,1,16,128]{4,3,2,1,0:T(8,128)S(1)} %get-tuple-element.37), channel_id=1, source_target_pairs={{0,4},{1,5},{2,6},{3,7},{4,8},{5,9},{6,10},{7,11},{8,12},{9,13},{1... | collective-permute-start | bytes 786440 | tf_op jit(solution)/shard_map/ppermute | solution.py:17
  19.1 12.6 %collective-permute-start.2 = (f32[2,16,16,1,128]{4,3,2,1,0:T(1,128)}, f32[2,16,16,1,128]{4,3,2,1,0:T(1,128)}, u32[]{:S(2)}, u32[]{:S(2)}) collective-permute-start(f32[2,16,16,1,128]{4,3,2,1,0:T(1,128)} %get-tuple-element.38), channel_id=1, source_target_pairs={{1,0},{2,1},{3,2},{4,3},{5,4},{6,5},{7,6},{8,7},{9,8},{10,9},{11,1... | collective-permute-start | bytes 786440 | tf_op jit(solution)/shard_map/ppermute | solution.py:17
  22.0 10.9 %collective-permute-start.3 = (f32[2,16,16,1,128]{4,3,2,1,0:T(1,128)}, f32[2,16,16,1,128]{4,3,2,1,0:T(1,128)}, u32[]{:S(2)}, u32[]{:S(2)}) collective-permute-start(f32[2,16,16,1,128]{4,3,2,1,0:T(1,128)} %get-tuple-element.39), channel_id=1, source_target_pairs={{0,1},{1,2},{2,3},{3,4},{4,5},{5,6},{6,7},{7,8},{8,9},{9,10},{10,1... | collective-permute-start | bytes 786440 | tf_op jit(solution)/shard_map/ppermute | solution.py:17
  48.9 13.9 %collective-permute-start.6 = (f32[2,16,16,1,128]{4,3,2,1,0:T(1,128)S(1)}, f32[2,16,16,1,128]{4,3,2,1,0:T(1,128)S(1)}, u32[]{:S(2)}, u32[]{:S(2)}) collective-permute-start(f32[2,16,16,1,128]{4,3,2,1,0:T(1,128)S(1)} %get-tuple-element.34), channel_id=1, source_target_pairs={{1,0},{2,1},{3,2},{4,3},{5,4},{6,5},{7,6},{8,7},{9,8},{10,9},{11,1... | collective-permute-start | bytes 786440 | tf_op jit(solution)/shard_map/ppermute | solution.py:17
  50.8 12.3 %collective-permute-start.7 = (f32[2,16,16,1,128]{4,3,2,1,0:T(1,128)S(1)}, f32[2,16,16,1,128]{4,3,2,1,0:T(1,128)S(1)}, u32[]{:S(2)}, u32[]{:S(2)}) collective-permute-start(f32[2,16,16,1,128]{4,3,2,1,0:T(1,128)S(1)} %get-tuple-element.35), channel_id=1, source_target_pairs={{0,1},{1,2},{2,3},{3,4},{4,5},{5,6},{6,7},{7,8},{8,9},{9,10},{10,1... | collective-permute-start | bytes 786440 | tf_op jit(solution)/shard_map/ppermute | solution.py:17
  55.2 16.6 %collective-permute-start.4 = (f32[2,16,1,16,128]{4,3,2,1,0:T(8,128)S(1)}, f32[2,16,1,16,128]{4,3,2,1,0:T(8,128)S(1)}, u32[]{:S(2)}, u32[]{:S(2)}) collective-permute-start(f32[2,16,1,16,128]{4,3,2,1,0:T(8,128)S(1)} %get-tuple-element.32), channel_id=1, source_target_pairs={{4,0},{5,1},{6,2},{7,3},{8,4},{9,5},{10,6},{11,7},{12,8},{13,9},{1... | collective-permute-start | bytes 786440 | tf_op jit(solution)/shard_map/ppermute | solution.py:17
  57.1 16.5 %collective-permute-start.5 = (f32[2,16,1,16,128]{4,3,2,1,0:T(8,128)S(1)}, f32[2,16,1,16,128]{4,3,2,1,0:T(8,128)S(1)}, u32[]{:S(2)}, u32[]{:S(2)}) collective-permute-start(f32[2,16,1,16,128]{4,3,2,1,0:T(8,128)S(1)} %get-tuple-element.33), channel_id=1, source_target_pairs={{0,4},{1,5},{2,6},{3,7},{4,8},{5,9},{6,10},{7,11},{8,12},{9,13},{1... | collective-permute-start | bytes 786440 | tf_op jit(solution)/shard_map/ppermute | solution.py:17
  87.4 15.5 %collective-permute-start.8 = (f32[2,16,1,8,128]{4,3,2,1,0:T(8,128)S(1)}, f32[2,16,1,8,128]{4,3,2,1,0:T(8,128)S(1)}, u32[]{:S(2)}, u32[]{:S(2)}) collective-permute-start(f32[2,16,1,8,128]{4,3,2,1,0:T(8,128)S(1)} %get-tuple-element.54), channel_id=1, source_target_pairs={{4,0},{5,1},{6,2},{7,3},{8,4},{9,5},{10,6},{11,7},{12,8},{13,9},{1... | collective-permute-start | bytes 393224 | tf_op jit(solution)/shard_map/ppermute | solution.py:17
  89.3 13.6 %collective-permute-start.9 = (f32[2,16,1,8,128]{4,3,2,1,0:T(8,128)S(1)}, f32[2,16,1,8,128]{4,3,2,1,0:T(8,128)S(1)}, u32[]{:S(2)}, u32[]{:S(2)}) collective-permute-start(f32[2,16,1,8,128]{4,3,2,1,0:T(8,128)S(1)} %get-tuple-element.55), channel_id=1, source_target_pairs={{0,4},{1,5},{2,6},{3,7},{4,8},{5,9},{6,10},{7,11},{8,12},{9,13},{1... | collective-permute-start | bytes 393224 | tf_op jit(solution)/shard_map/ppermute | solution.py:17
  95.3 6.3 %collective-permute-start.10 = (f32[2,16,8,1,128]{4,3,2,1,0:T(1,128)S(1)}, f32[2,16,8,1,128]{4,3,2,1,0:T(1,128)S(1)}, u32[]{:S(2)}, u32[]{:S(2)}) collective-permute-start(f32[2,16,8,1,128]{4,3,2,1,0:T(1,128)S(1)} %get-tuple-element.56), channel_id=1, source_target_pairs={{1,0},{2,1},{3,2},{4,3},{5,4},{6,5},{7,6},{8,7},{9,8},{10,9},{11,1... | collective-permute-start | bytes 393224 | tf_op jit(solution)/shard_map/ppermute | solution.py:17
  97.5 5.3 %collective-permute-start.11 = (f32[2,16,8,1,128]{4,3,2,1,0:T(1,128)S(1)}, f32[2,16,8,1,128]{4,3,2,1,0:T(1,128)S(1)}, u32[]{:S(2)}, u32[]{:S(2)}) collective-permute-start(f32[2,16,8,1,128]{4,3,2,1,0:T(1,128)S(1)} %get-tuple-element.57), channel_id=1, source_target_pairs={{0,1},{1,2},{2,3},{3,4},{4,5},{5,6},{6,7},{7,8},{8,9},{9,10},{10,1... | collective-permute-start | bytes 393224 | tf_op jit(solution)/shard_map/ppermute | solution.py:17
  104.4 16.3 %collective-permute-start.12 = (f32[2,16,1,8,128]{4,3,2,1,0:T(8,128)S(1)}, f32[2,16,1,8,128]{4,3,2,1,0:T(8,128)S(1)}, u32[]{:S(2)}, u32[]{:S(2)}) collective-permute-start(f32[2,16,1,8,128]{4,3,2,1,0:T(8,128)S(1)} %get-tuple-element.50), channel_id=1, source_target_pairs={{4,0},{5,1},{6,2},{7,3},{8,4},{9,5},{10,6},{11,7},{12,8},{13,9},{1... | collective-permute-start | bytes 393224 | tf_op jit(solution)/shard_map/ppermute | solution.py:17
  106.3 14.4 %collective-permute-start.13 = (f32[2,16,1,8,128]{4,3,2,1,0:T(8,128)S(1)}, f32[2,16,1,8,128]{4,3,2,1,0:T(8,128)S(1)}, u32[]{:S(2)}, u32[]{:S(2)}) collective-permute-start(f32[2,16,1,8,128]{4,3,2,1,0:T(8,128)S(1)} %get-tuple-element.51), channel_id=1, source_target_pairs={{0,4},{1,5},{2,6},{3,7},{4,8},{5,9},{6,10},{7,11},{8,12},{9,13},{1... | collective-permute-start | bytes 393224 | tf_op jit(solution)/shard_map/ppermute | solution.py:17
  111.8 7.6 %collective-permute-start.14 = (f32[2,16,8,1,128]{4,3,2,1,0:T(1,128)S(1)}, f32[2,16,8,1,128]{4,3,2,1,0:T(1,128)S(1)}, u32[]{:S(2)}, u32[]{:S(2)}) collective-permute-start(f32[2,16,8,1,128]{4,3,2,1,0:T(1,128)S(1)} %get-tuple-element.52), channel_id=1, source_target_pairs={{1,0},{2,1},{3,2},{4,3},{5,4},{6,5},{7,6},{8,7},{9,8},{10,9},{11,1... | collective-permute-start | bytes 393224 | tf_op jit(solution)/shard_map/ppermute | solution.py:17
  115.2 5.3 %collective-permute-start.15 = (f32[2,16,8,1,128]{4,3,2,1,0:T(1,128)S(1)}, f32[2,16,8,1,128]{4,3,2,1,0:T(1,128)S(1)}, u32[]{:S(2)}, u32[]{:S(2)}) collective-permute-start(f32[2,16,8,1,128]{4,3,2,1,0:T(1,128)S(1)} %get-tuple-element.53), channel_id=1, source_target_pairs={{0,1},{1,2},{2,3},{3,4},{4,5},{5,6},{6,7},{7,8},{8,9},{9,10},{10,1... | collective-permute-start | bytes 393224 | tf_op jit(solution)/shard_map/ppermute | solution.py:17
  122.0 16.3 %collective-permute-start.16 = (f32[2,16,1,8,128]{4,3,2,1,0:T(8,128)S(1)}, f32[2,16,1,8,128]{4,3,2,1,0:T(8,128)S(1)}, u32[]{:S(2)}, u32[]{:S(2)}) collective-permute-start(f32[2,16,1,8,128]{4,3,2,1,0:T(8,128)S(1)} %get-tuple-element.46), channel_id=1, source_target_pairs={{4,0},{5,1},{6,2},{7,3},{8,4},{9,5},{10,6},{11,7},{12,8},{13,9},{1... | collective-permute-start | bytes 393224 | tf_op jit(solution)/shard_map/ppermute | solution.py:17
  123.9 14.4 %collective-permute-start.17 = (f32[2,16,1,8,128]{4,3,2,1,0:T(8,128)S(1)}, f32[2,16,1,8,128]{4,3,2,1,0:T(8,128)S(1)}, u32[]{:S(2)}, u32[]{:S(2)}) collective-permute-start(f32[2,16,1,8,128]{4,3,2,1,0:T(8,128)S(1)} %get-tuple-element.47), channel_id=1, source_target_pairs={{0,4},{1,5},{2,6},{3,7},{4,8},{5,9},{6,10},{7,11},{8,12},{9,13},{1... | collective-permute-start | bytes 393224 | tf_op jit(solution)/shard_map/ppermute | solution.py:17
  129.4 7.6 %collective-permute-start.18 = (f32[2,16,8,1,128]{4,3,2,1,0:T(1,128)S(1)}, f32[2,16,8,1,128]{4,3,2,1,0:T(1,128)S(1)}, u32[]{:S(2)}, u32[]{:S(2)}) collective-permute-start(f32[2,16,8,1,128]{4,3,2,1,0:T(1,128)S(1)} %get-tuple-element.48), channel_id=1, source_target_pairs={{1,0},{2,1},{3,2},{4,3},{5,4},{6,5},{7,6},{8,7},{9,8},{10,9},{11,1... | collective-permute-start | bytes 393224 | tf_op jit(solution)/shard_map/ppermute | solution.py:17
  132.9 5.3 %collective-permute-start.19 = (f32[2,16,8,1,128]{4,3,2,1,0:T(1,128)S(1)}, f32[2,16,8,1,128]{4,3,2,1,0:T(1,128)S(1)}, u32[]{:S(2)}, u32[]{:S(2)}) collective-permute-start(f32[2,16,8,1,128]{4,3,2,1,0:T(1,128)S(1)} %get-tuple-element.49), channel_id=1, source_target_pairs={{0,1},{1,2},{2,3},{3,4},{4,5},{5,6},{6,7},{7,8},{8,9},{9,10},{10,1... | collective-permute-start | bytes 393224 | tf_op jit(solution)/shard_map/ppermute | solution.py:17
  149.3 13.8 %collective-permute-start.22 = (f32[2,16,16,1,128]{4,3,2,1,0:T(1,128)S(1)}, f32[2,16,16,1,128]{4,3,2,1,0:T(1,128)S(1)}, u32[]{:S(2)}, u32[]{:S(2)}) collective-permute-start(f32[2,16,16,1,128]{4,3,2,1,0:T(1,128)S(1)} %get-tuple-element.30), channel_id=1, source_target_pairs={{1,0},{2,1},{3,2},{4,3},{5,4},{6,5},{7,6},{8,7},{9,8},{10,9},{11,1... | collective-permute-start | bytes 786440 | tf_op jit(solution)/shard_map/ppermute | solution.py:17
  152.3 11.1 %collective-permute-start.23 = (f32[2,16,16,1,128]{4,3,2,1,0:T(1,128)S(1)}, f32[2,16,16,1,128]{4,3,2,1,0:T(1,128)S(1)}, u32[]{:S(2)}, u32[]{:S(2)}) collective-permute-start(f32[2,16,16,1,128]{4,3,2,1,0:T(1,128)S(1)} %get-tuple-element.31), channel_id=1, source_target_pairs={{0,1},{1,2},{2,3},{3,4},{4,5},{5,6},{6,7},{7,8},{8,9},{9,10},{10,1... | collective-permute-start | bytes 786440 | tf_op jit(solution)/shard_map/ppermute | solution.py:17
  155.7 16.5 %collective-permute-start.20 = (f32[2,16,1,16,128]{4,3,2,1,0:T(8,128)S(1)}, f32[2,16,1,16,128]{4,3,2,1,0:T(8,128)S(1)}, u32[]{:S(2)}, u32[]{:S(2)}) collective-permute-start(f32[2,16,1,16,128]{4,3,2,1,0:T(8,128)S(1)} %get-tuple-element.28), channel_id=1, source_target_pairs={{4,0},{5,1},{6,2},{7,3},{8,4},{9,5},{10,6},{11,7},{12,8},{13,9},{1... | collective-permute-start | bytes 786440 | tf_op jit(solution)/shard_map/ppermute | solution.py:17
  157.6 16.9 %collective-permute-start.21 = (f32[2,16,1,16,128]{4,3,2,1,0:T(8,128)S(1)}, f32[2,16,1,16,128]{4,3,2,1,0:T(8,128)S(1)}, u32[]{:S(2)}, u32[]{:S(2)}) collective-permute-start(f32[2,16,1,16,128]{4,3,2,1,0:T(8,128)S(1)} %get-tuple-element.29), channel_id=1, source_target_pairs={{0,4},{1,5},{2,6},{3,7},{4,8},{5,9},{6,10},{7,11},{8,12},{9,13},{1... | collective-permute-start | bytes 786440 | tf_op jit(solution)/shard_map/ppermute | solution.py:17
  (11 other events, 92.4 us)
where the time goes:
time: 183 us; the launch traced here: 182 us
  starting transfers between devices  83.3 us (46%)
  other arithmetic  62.6 us (34%)
  waiting for transfers between devices  26.2 us (14%)
  local copies, waits for them, and re-layouts  9.31 us (5%)
    ppermute x24, starting transfers between devices, passed_along(): lax.ppermute(value, axis, [(source, source + steps) for source in range(l...  83.3 us
    ppermute x24, waiting for transfers between devices, passed_along(): lax.ppermute(value, axis, [(source, source + steps) for source in range(l...  26.2 us
    add x6, other arithmetic, tile_operator(): near = weight_x * (along_x + along_y) + along_z  19.3 us
    broadcast_in_dim x2, local copies, waits for them, and re-layouts, refine(): return jnp.repeat(jnp.repeat(field, 2, axis=-3), 2, axis=-2)  6.66 us
    another operation x16, other arithmetic, relax(): return jnp.stack([real, imag])  6.25 us
    add x5, other arithmetic, relax(): real = field[0] + OMEGA * (inv_r * rest_r - inv_i * rest_i)  5.33 us
    sub x1, other arithmetic, shards(): rest = rhs - tile_operator(field, fine_faces(field), fine_r, fine_i, 1.0)  5.13 us
    mul x4, other arithmetic, shards(): hit_x[:, :, None, None] * hit_y[:, None, :, None] * hit_z[:, None, None, :]  4.48 us
  transfers between devices with their start and end apart: 24, of which 10 were waited for; matrix products, arithmetic and copies ran while one was open for 7% of the time, Pallas kernels for 0%

commit v1 on v0

v1 whole, which is shorter than its diff:
```python
import functools

import jax
import jax.numpy as jnp
from jax import lax
from jax.experimental import pallas as pl
from jax.experimental.pallas import tpu as pltpu
from jax.sharding import PartitionSpec as P

TY = 4
OMEGA = 0.8
BETA = 0.5
B = 16
C = 8
Z = 128
F32 = jnp.float32
UNROLL = 4
PARTS = 2
FACE_STRIDE = 2 * B + 8
STRIDE = B * B + 8
Y_COUNT = (14, 12, 10, 8)
Y_START = (0, 14, 26, 36)


def z_sum(u):
    lane = lax.broadcasted_iota(jnp.int32, u.shape, 1)
    low = jnp.where(lane == 0, 0.0, pltpu.roll(u, 1, 1))
    high = jnp.where(lane == Z - 1, 0.0, pltpu.roll(u, Z - 1, 1))
    return low + high


def weight(k, centre):
    real = centre - k
    imag = BETA * k
    scale = jnp.where(k > 0.0, OMEGA / (real * real + imag * imag), 0.0)
    return real * scale, -imag * scale


def times(w_r, w_i, r, i):
    return w_r * r - w_i * i, w_r * i + w_i * r


def row_of(ref, c, x, y, shots):
    return jnp.broadcast_to(ref[c, x, pl.ds(y, 1), :], (shots, Z))


def sides_of(ref, c, x, y):
    return (ref[c, x - 1, y] + ref[c, x + 1, y]) + (ref[c, x, y - 1] + ref[c, x, y + 1])


def near(ref, cells):
    along = [z_sum(ref[c, x, y]) for x, y in cells for c in range(2)]
    return [[along[2 * n + c] + sides_of(ref, c, x, y) for c in range(2)] for n, (x, y) in enumerate(cells)]


def place():
    tile = lax.axis_index("space")
    return tile // TY, tile % TY


def sources(cell_ref, amp_ref, start, shots):
    sub = lax.broadcasted_iota(jnp.int32, (shots, Z), 0)
    lane = lax.broadcasted_iota(jnp.int32, (shots, Z), 1)
    cell = jnp.zeros((shots, Z), jnp.int32)
    amp_r = jnp.zeros((shots, Z), F32)
    amp_i = jnp.zeros((shots, Z), F32)
    for s in range(shots):
        cell = jnp.where(sub == s, cell_ref[start + s], cell)
        amp_r = jnp.where(sub == s, amp_ref[0, start + s], amp_r)
        amp_i = jnp.where(sub == s, amp_ref[1, start + s], amp_i)
    return cell - lane, amp_r, amp_i


def with_source(source, row, column, x, y, r, i):
    spot, amp_r, amp_i = source
    hit = spot == ((row * B + x) * (TY * B) + column * B + y) * Z
    return r + jnp.where(hit, amp_r, 0.0), i + jnp.where(hit, amp_i, 0.0)


def coarse_k(k2_ref, x):
    total = k2_ref[2 * x, pl.ds(0, C, stride=2), :] + k2_ref[2 * x + 1, pl.ds(0, C, stride=2), :]
    total = total + k2_ref[2 * x, pl.ds(1, C, stride=2), :] + k2_ref[2 * x + 1, pl.ds(1, C, stride=2), :]
    return 0.25 * total


def start_all(copies):
    for copy in copies:
        copy.start()
    return copies


def small_copies(pairs, sems):
    return [pltpu.make_async_copy(source, target, sems.at[n]) for n, (source, target) in enumerate(pairs)]


def faces_kernel(start, shots, cell_in, amp_in, raw_ref, k2_in, x0_ref, x1_ref, cell_ref, amp_ref, k2_ref, low_ref, high_ref, sems):
    width = 2 * B
    mine = pl.ds(start, shots)
    copies = small_copies(
        [
            (raw_ref.at[:, mine, pl.ds(0, width)], low_ref.at[:, :, pl.ds(0, width)]),
            (raw_ref.at[:, mine, pl.ds(B * B - width, width)], high_ref.at[:, :, pl.ds(0, width)]),
            (cell_in, cell_ref),
            (amp_in, amp_ref),
            (k2_in, k2_ref),
        ],
        sems,
    )
    for copy in start_all(copies):
        copy.wait()
    row, column = place()
    even = row % 2 == 0
    source = sources(cell_ref, amp_ref, start, shots)
    base = 64 * shots
    if start == 0:
        k_low, k_high = k2_ref[0], k2_ref[B - 1]
        x0_ref[pl.ds(base, B), :] = jnp.where(even, k_high, k_low)
        x1_ref[pl.ds(base, B), :] = jnp.where(even, k_low, k_high)
        for d in range(3):
            k_low, k_high = coarse_k(k2_ref, d), coarse_k(k2_ref, C - 1 - d)
            x0_ref[pl.ds(base + B + d * C, C), :] = jnp.where(even, k_high, k_low)
            x1_ref[pl.ds(base + B + d * C, C), :] = jnp.where(even, k_low, k_high)
    low = low_ref.reshape(2, shots * FACE_STRIDE, Z)
    high = high_ref.reshape(2, shots * FACE_STRIDE, Z)
    for d in range(2):
        lw_r, lw_i = weight(k2_ref[d], 6.0)
        hw_r, hw_i = weight(k2_ref[B - 1 - d], 6.0)
        for y in range(B):
            values = []
            for side, local, x, w_r, w_i in ((low, d, d, lw_r, lw_i), (high, 1 - d, B - 1 - d, hw_r, hw_i)):
                r, i = (side[c, pl.ds(local * B + y, shots, stride=FACE_STRIDE), :] for c in range(2))
                r, i = with_source(source, row, column, x, y, r, i)
                values.append(times(w_r[y : y + 1], w_i[y : y + 1], r, i))
            for c in range(2):
                at = pl.ds(((d * B + y) * 2 + c) * shots, shots)
                x0_ref[at, :] = jnp.where(even, values[1][c], values[0][c])
                x1_ref[at, :] = jnp.where(even, values[0][c], values[1][c])


def first_coarse(shots, v_ref, cb_ref, cw_ref, e_ref, cells):
    blocks, rings = [], []
    for x, y in cells:
        fx, fy = 2 * x + 1, 2 * y + 1
        for c in range(2):
            blocks.append((v_ref[c, fx, fy] + v_ref[c, fx + 1, fy]) + (v_ref[c, fx, fy + 1] + v_ref[c, fx + 1, fy + 1]))
            ring = (v_ref[c, fx - 1, fy] + v_ref[c, fx - 1, fy + 1]) + (v_ref[c, fx + 2, fy] + v_ref[c, fx + 2, fy + 1])
            rings.append(ring + (v_ref[c, fx, fy - 1] + v_ref[c, fx + 1, fy - 1]) + (v_ref[c, fx, fy + 2] + v_ref[c, fx + 1, fy + 2]))
    along = [z_sum(block) for block in blocks]
    for n, (x, y) in enumerate(cells):
        r, i = (cb_ref[c, x, y] + 0.25 * (2.0 * blocks[2 * n + c] + rings[2 * n + c] + along[2 * n + c]) for c in range(2))
        r, i = times(row_of(cw_ref, 0, x, y, shots), row_of(cw_ref, 1, x, y, shots), r, i)
        e_ref[0, x + 4, y + 4] = r
        e_ref[1, x + 4, y + 4] = i


def second_v(shots, u_ref, w_ref, v_ref, cells):
    sums = near(u_ref, [(x + 2, y + 2) for x, y in cells])
    for (x, y), (r, i) in zip(cells, sums):
        r, i = times(row_of(w_ref, 0, x + 1, y + 1, shots), row_of(w_ref, 1, x + 1, y + 1, shots), r, i)
        v_ref[0, x + 1, y + 1] = 0.4 * u_ref[0, x + 2, y + 2] + r
        v_ref[1, x + 1, y + 1] = 0.4 * u_ref[1, x + 2, y + 2] + i


def inner_kernel(start, shots, cell_in, amp_in, raw_ref, k2_in, u_ref, v_ref, e_ref, cb_ref, w_ref, cw_ref, cell_ref, amp_ref, k2_ref, held_ref, sems):
    rows = [pl.ds(part * (B * B // 4), B * B // 4) for part in range(4)]
    pairs = [(cell_in, cell_ref), (amp_in, amp_ref), (k2_in, k2_ref)]
    pairs += [(raw_ref.at[:, pl.ds(start, shots), at], held_ref.at[:, :, at]) for at in rows]
    copies = start_all(small_copies(pairs, sems))
    for copy in copies[:3]:
        copy.wait()
    row, column = place()
    source = sources(cell_ref, amp_ref, start, shots)
    raw = held_ref.reshape(2, shots * STRIDE, Z)

    def first(x):
        cw_r, cw_i = weight(coarse_k(k2_ref, x), 3.0)
        cw_ref[0, x] = cw_r
        cw_ref[1, x] = cw_i
        for half in range(2):
            w_r, w_i = weight(k2_ref[2 * x + half], 6.0)
            w_ref[0, 2 * x + half + 1, pl.ds(1, B), :] = w_r
            w_ref[1, 2 * x + half + 1, pl.ds(1, B), :] = w_i
        for y in range(C):
            total = [None, None]
            for half in range(2):
                for other in range(2):
                    fx, fy = 2 * x + half, 2 * y + other
                    r, i = (raw[c, pl.ds(fx * B + fy, shots, stride=STRIDE), :] for c in range(2))
                    r, i = with_source(source, row, column, fx, fy, r, i)
                    total = [r, i] if total[0] is None else [total[0] + r, total[1] + i]
                    w_r = row_of(w_ref, 0, fx + 1, fy + 1, shots)
                    w_i = row_of(w_ref, 1, fx + 1, fy + 1, shots)
                    r, i = times(w_r, w_i, r, i)
                    u_ref[0, fx + 2, fy + 2] = r
                    u_ref[1, fx + 2, fy + 2] = i
            cb_ref[0, x, y] = 0.01 * total[0]
            cb_ref[1, x, y] = 0.01 * total[1]

    for part in range(4):
        copies[3 + part].wait()
        pl.loop(2 * part, 2 * part + 2)(first)

    @pl.loop(1, B - 1, unroll=2)
    def _(x):
        second_v(shots, u_ref, w_ref, v_ref, [(x, y) for y in range(1, B - 1)])

    @pl.loop(1, C - 1, unroll=3)
    def _(x):
        first_coarse(shots, v_ref, cb_ref, cw_ref, e_ref, [(x, y) for y in range(1, C - 1)])


def y_faces_kernel(start, shots, x0_ref, x1_ref, u_ref, k2_ref, y0_ref, y1_ref):
    row, column = place()
    even = row % 2 == 0
    flag = column % 2
    base = 68 * shots
    coarse_base = 64 * shots + B
    for out, high in ((y0_ref, flag == 0), (y1_ref, flag == 1)):
        y = jnp.where(high, B - 1, 0)
        for c in range(2):
            at = pl.ds(pl.multiple_of((y * 2 + c) * shots, 8), shots)
            first, second = x0_ref[at, :], x1_ref[at, :]
            out[pl.ds(c * shots, shots), :] = jnp.where(even, second, first)
            out[pl.ds((17 * 2 + c) * shots, shots), :] = jnp.where(even, first, second)
        for d in range(2):
            from_y = jnp.where(high, B - 1 - d, d) + 2
            at = 1 if d == 0 else 18
            for x in range(B):
                for c in range(2):
                    out[pl.ds(((at + x) * 2 + c) * shots, shots), :] = u_ref[c, x + 2, from_y]
        if start > 0:
            continue
        out[pl.ds(base, B), :] = jnp.where(high, k2_ref[:, B - 1, :], k2_ref[:, 0, :])
        rows = [coarse_k(k2_ref, x) for x in range(C)]
        for d in range(3):
            at = base + B + d * 16
            for h in range(3):
                first = x0_ref[pl.ds(coarse_base + h * C, C), :]
                second = x1_ref[pl.ds(coarse_base + h * C, C), :]
                for position, halo in ((2 - h, jnp.where(even, second, first)), (11 + h, jnp.where(even, first, second))):
                    out[pl.ds(at + position, 1), :] = jnp.where(high, halo[C - 1 - d : C - d], halo[d : d + 1])
            for x in range(C):
                out[pl.ds(at + 3 + x, 1), :] = jnp.where(high, rows[x][C - 1 - d : C - d], rows[x][d : d + 1])
            out[pl.ds(at + 14, 2), :] = jnp.zeros((2, Z), F32)


def ring_kernel(start, shots, x0_ref, x1_ref, y0_ref, y1_ref, cb_ref, cw_ref, u_in, v_in, e_in, w_in, u_ref, v_ref, e_ref, w_ref, ex0_ref, ex1_ref):
    del u_in, v_in, e_in, w_in
    row, column = place()
    flag_x, flag_y = row % 2, column % 2
    for message, high in ((x0_ref, flag_x == 0), (x1_ref, flag_x == 1)):
        for d in range(2):
            to = jnp.where(high, B + 2 + d, 1 - d)
            for y in range(B):
                for c in range(2):
                    u_ref[c, to, y + 2] = message[pl.ds(((d * B + y) * 2 + c) * shots, shots), :]
        if start > 0:
            continue
        w_r, w_i = weight(message[pl.ds(64 * shots, B), :], 6.0)
        to = jnp.where(high, B + 1, 0)
        w_ref[0, to, pl.ds(1, B), :] = w_r
        w_ref[1, to, pl.ds(1, B), :] = w_i
    for message, high in ((y0_ref, flag_y == 0), (y1_ref, flag_y == 1)):
        for d in range(2):
            to = jnp.where(high, B + 2 + d, 1 - d)
            at, first, count = ((0, 1, 18), (18, 2, 16))[d]
            for x in range(count):
                for c in range(2):
                    u_ref[c, first + x, to] = message[pl.ds(((at + x) * 2 + c) * shots, shots), :]
        if start > 0:
            continue
        w_r, w_i = weight(message[pl.ds(68 * shots, B), :], 6.0)
        to = jnp.where(high, B + 1, 0)
        for x in range(B):
            w_ref[0, x + 1, pl.ds(to, 1), :] = w_r[x : x + 1]
            w_ref[1, x + 1, pl.ds(to, 1), :] = w_i[x : x + 1]

    @pl.loop(0, B, unroll=UNROLL)
    def _(y):
        second_v(shots, u_ref, w_ref, v_ref, [(x, y) for x in (-1, 0, B - 1, B)])

    @pl.loop(0, B, unroll=UNROLL)
    def _(x):
        second_v(shots, u_ref, w_ref, v_ref, [(x, y) for y in (-1, 0, B - 1, B)])

    @pl.loop(0, C, unroll=UNROLL)
    def _(y):
        first_coarse(shots, v_ref, cb_ref, cw_ref, e_ref, [(x, y) for x in (0, C - 1)])

    @pl.loop(1, C - 1, unroll=3)
    def _(x):
        first_coarse(shots, v_ref, cb_ref, cw_ref, e_ref, [(x, y) for y in (0, C - 1)])

    for out, high in ((ex0_ref, flag_x == 0), (ex1_ref, flag_x == 1)):
        for d in range(4):
            x = jnp.where(high, C - 1 - d, d) + 4
            for y in range(C):
                for c in range(2):
                    out[pl.ds(((d * C + y) * 2 + c) * shots, shots), :] = e_ref[c, x, y + 4]


def weights_kernel(shots, x0_ref, x1_ref, y0_ref, y1_ref, k2_ref, cwh_ref):
    row, column = place()
    flag_x, flag_y = row % 2, column % 2
    for x in range(C):
        cw_r, cw_i = weight(coarse_k(k2_ref, x), 3.0)
        cwh_ref[0, x + 3, pl.ds(3, C), :] = cw_r
        cwh_ref[1, x + 3, pl.ds(3, C), :] = cw_i
    for message, high in ((x0_ref, flag_x == 0), (x1_ref, flag_x == 1)):
        for d in range(3):
            to = jnp.where(high, C + 3 + d, 2 - d)
            cw_r, cw_i = weight(message[pl.ds(64 * shots + B + d * C, C), :], 3.0)
            cwh_ref[0, to, pl.ds(3, C), :] = cw_r
            cwh_ref[1, to, pl.ds(3, C), :] = cw_i
    for message, high in ((y0_ref, flag_y == 0), (y1_ref, flag_y == 1)):
        for d in range(3):
            to = jnp.where(high, C + 3 + d, 2 - d)
            cw_r, cw_i = weight(message[pl.ds(68 * shots + B + d * 16, 16), :], 3.0)
            for x in range(14):
                cwh_ref[0, x, pl.ds(to, 1), :] = cw_r[x : x + 1]
                cwh_ref[1, x, pl.ds(to, 1), :] = cw_i[x : x + 1]


def base_kernel(shots, u_ref, v_ref, w_ref, g_ref):
    @pl.loop(0, B, unroll=2)
    def _(x):
        sums = near(v_ref, [(x + 1, y + 1) for y in range(B)])
        for y, (r, i) in enumerate(sums):
            r, i = times(row_of(w_ref, 0, x + 1, y + 1, shots), row_of(w_ref, 1, x + 1, y + 1, shots), r, i)
            g_ref[0, x, y] = v_ref[0, x + 1, y + 1] + 0.84 * u_ref[0, x + 2, y + 2] + r
            g_ref[1, x, y] = v_ref[1, x + 1, y + 1] + 0.84 * u_ref[1, x + 2, y + 2] + i


def coarse_y_kernel(shots, ex0_ref, ex1_ref, e_in, e_ref, ey0_ref, ey1_ref):
    del e_in
    row, column = place()
    flag_x, flag_y = row % 2, column % 2
    for message, high in ((ex0_ref, flag_x == 0), (ex1_ref, flag_x == 1)):
        for d in range(4):
            to = jnp.where(high, C + 4 + d, 3 - d)
            for y in range(C):
                for c in range(2):
                    e_ref[c, to, y + 4] = message[pl.ds(((d * C + y) * 2 + c) * shots, shots), :]
    for out, high in ((ey0_ref, flag_y == 0), (ey1_ref, flag_y == 1)):
        for d in range(4):
            y = jnp.where(high, C - 1 - d, d) + 4
            for n in range(Y_COUNT[d]):
                for c in range(2):
                    out[pl.ds(((Y_START[d] + n) * 2 + c) * shots, shots), :] = e_ref[c, 1 + d + n, y]


def final_kernel(start, shots, ey0_ref, ey1_ref, cwh_ref, w_ref, g_ref, *refs):
    e_ref, out_ref, e2_ref, e3_ref, stage_ref, sems = refs[-6:]
    row, column = place()
    flag_y = column % 2
    for message, high in ((ey0_ref, flag_y == 0), (ey1_ref, flag_y == 1)):
        for d in range(4):
            to = jnp.where(high, C + 4 + d, 3 - d)
            for n in range(Y_COUNT[d]):
                for c in range(2):
                    e_ref[c, 1 + d + n, to] = message[pl.ds(((Y_START[d] + n) * 2 + c) * shots, shots), :]
    stage = stage_ref.reshape(2, shots * STRIDE, Z)

    def sweep(old, new, x, reach_y):
        cells = range(-reach_y, C + reach_y)
        along = [z_sum(old[c, x + 4, y + 4]) for y in cells for c in range(2)]
        for n, y in enumerate(cells):
            parts = []
            for c in range(2):
                sides = (old[c, x + 3, y + 4] + old[c, x + 5, y + 4]) + (old[c, x + 4, y + 3] + old[c, x + 4, y + 5])
                parts.append(0.25 * sides + along[2 * n + c])
            w_r, w_i = row_of(cwh_ref, 0, x + 3, y + 3, shots), row_of(cwh_ref, 1, x + 3, y + 3, shots)
            parts = times(w_r, w_i, *parts)
            for c in range(2):
                new[c, x + 4, y + 4] = 0.2 * old[c, x + 4, y + 4] + e_ref[c, x + 4, y + 4] + parts[c]

    for old, new, reach in ((e_ref, e2_ref, 3), (e2_ref, e3_ref, 2), (e3_ref, e2_ref, 1)):

        @pl.loop(0, C, unroll=UNROLL)
        def _(x, old=old, new=new, reach=reach):
            sweep(old, new, x, reach)

        for d in range(1, reach + 1):
            for x in (-d, C - 1 + d):
                sweep(old, new, x, reach - d)

    def finish(x):
        along = [z_sum(e2_ref[c, x + 4, y + 4]) for y in range(C) for c in range(2)]
        for y in range(C):
            e = [e2_ref[c, x + 4, y + 4] for c in range(2)]
            near_x = [[e2_ref[c, x + 3 + 2 * half, y + 4] for c in range(2)] for half in range(2)]
            near_y = [[e2_ref[c, x + 4, y + 3 + 2 * half] for c in range(2)] for half in range(2)]
            middle = [2.0 * e[c] + along[2 * y + c] for c in range(2)]
            for half in range(2):
                total = [middle[c] + near_x[half][c] for c in range(2)]
                for other in range(2):
                    fx, fy = 2 * x + half, 2 * y + other
                    w_r, w_i = row_of(w_ref, 0, fx + 1, fy + 1, shots), row_of(w_ref, 1, fx + 1, fy + 1, shots)
                    change = times(w_r, w_i, total[0] + near_y[other][0], total[1] + near_y[other][1])
                    for c in range(2):
                        value = g_ref[c, fx, fy] + 0.2 * e[c] + change[c]
                        stage[c, pl.ds(fx * B + fy, shots, stride=STRIDE), :] = value

    copies = []
    for part in range(PARTS):
        width = C // PARTS
        pl.loop(part * width, (part + 1) * width, unroll=min(UNROLL, width))(finish)
        rows = pl.ds(part * (B * B // PARTS), B * B // PARTS)
        copy = pltpu.make_async_copy(stage_ref.at[:, :, rows], out_ref.at[:, pl.ds(start, shots), rows], sems.at[part])
        copy.start()
        copies.append(copy)
    for copy in copies:
        copy.wait()


def call(kernel, inputs, outs, *, aliases={}, scratch=(), limit=16, flops=1, moved=1, out_any=()):
    spaces = {"h": pltpu.HBM, "r": pltpu.VMEM}
    return pl.pallas_call(
        kernel,
        in_specs=[pl.BlockSpec(memory_space=spaces[kind]) for kind, _ in inputs],
        out_specs=[pl.BlockSpec(memory_space=spaces["h" if n in out_any else "r"]) for n in range(len(outs))],
        out_shape=[jax.ShapeDtypeStruct(shape, F32) if n in out_any else pltpu.VMEM(shape, F32) for n, shape in enumerate(outs)],
        input_output_aliases=aliases,
        scratch_shapes=list(scratch),
        compiler_params=pltpu.CompilerParams(vmem_limit_bytes=limit * 1024 * 1024),
        cost_estimate=pl.CostEstimate(flops=flops, bytes_accessed=moved, transcendentals=0),
    )(*[pltpu.with_memory_space_constraint(value, spaces[kind]) for kind, value in inputs])


def swaps(pairs):
    return [pair for a, b in pairs for pair in ((a, b), (b, a))]


X0 = swaps([(t, t + TY) for t in range(16) if (t // TY) % 2 == 0])
X1 = swaps([(t, t + TY) for t in range(TY, 2 * TY)])
Y0 = swaps([(t, t + 1) for t in range(0, 16, 2)])
Y1 = swaps([(t, t + 1) for t in range(1, 16, TY)])


def swap(first, first_pairs, second, second_pairs):
    first = lax.ppermute(first, "space", first_pairs)
    second = lax.ppermute(second, "space", second_pairs)
    return first, second


SHOTS = 8
dma = pltpu.SemaphoreType.DMA
U_SHAPE = (2, B + 4, B + 4, SHOTS, Z)
V_SHAPE = (2, B + 2, B + 2, SHOTS, Z)
W_SHAPE = (2, B + 2, B + 2, Z)
E_SHAPE = (2, 2 * C, 2 * C, SHOTS, Z)
part = functools.partial


def small(total):
    return [pltpu.SMEM((total,), jnp.int32), pltpu.SMEM((2, total), F32), pltpu.VMEM((B, B, Z), F32)]


def faces(start, raw, k2, cell, amp):
    return call(
        part(faces_kernel, start, SHOTS),
        [("h", cell), ("h", amp), ("h", raw), ("h", k2)],
        [(64 * SHOTS + (0 if start else 40), Z)] * 2,
        scratch=small(cell.shape[0]) + [pltpu.VMEM((2, SHOTS, FACE_STRIDE, Z), F32)] * 2 + [dma((5,))],
    )


def inner(start, raw, k2, cell, amp):
    return call(
        part(inner_kernel, start, SHOTS),
        [("h", cell), ("h", amp), ("h", raw), ("h", k2)],
        [U_SHAPE, V_SHAPE, E_SHAPE, (2, C, C, SHOTS, Z), W_SHAPE, (2, C, C, Z)],
        scratch=small(cell.shape[0]) + [pltpu.VMEM((2, SHOTS, STRIDE, Z), F32), dma((7,))],
    )


def y_faces(start, x0, x1, u, k2):
    return call(
        part(y_faces_kernel, start, SHOTS),
        [("r", x0), ("r", x1), ("r", u), ("r", k2)],
        [(68 * SHOTS + (0 if start else 64), Z)] * 2,
    )


def ring(start, x0, x1, y0, y1, cb, cw, u, v, e, w):
    inputs = [("r", value) for value in (x0, x1, y0, y1, cb, cw, u, v, e, w)]
    return call(
        part(ring_kernel, start, SHOTS),
        inputs,
        [U_SHAPE, V_SHAPE, E_SHAPE, W_SHAPE, (64 * SHOTS, Z), (64 * SHOTS, Z)],
        aliases={6: 0, 7: 1, 8: 2, 9: 3},
    )


def weights(x0, x1, y0, y1, k2):
    inputs = [("r", value) for value in (x0, x1, y0, y1, k2)]
    return call(part(weights_kernel, SHOTS), inputs, [(2, 14, 14, Z)])[0]


def base(u, v, w):
    return call(part(base_kernel, SHOTS), [("r", u), ("r", v), ("r", w)], [(2, B, B, SHOTS, Z)])[0]


def coarse_y(ex0, ex1, e):
    return call(
        part(coarse_y_kernel, SHOTS),
        [("r", ex0), ("r", ex1), ("r", e)],
        [E_SHAPE, (88 * SHOTS, Z), (88 * SHOTS, Z)],
        aliases={2: 0},
    )


def final(start, ey0, ey1, cwh, w, g, e, out):
    total = 2 * SHOTS
    inputs = [("r", value) for value in (ey0, ey1, cwh, w, g, e)] + ([] if out is None else [("h", out)])
    return call(
        part(final_kernel, start, SHOTS),
        inputs,
        [E_SHAPE, (2, total, B * B, Z)],
        aliases={5: 0} if out is None else {5: 0, 6: 1},
        out_any=(1,),
        scratch=[pltpu.VMEM(E_SHAPE, F32), pltpu.VMEM(E_SHAPE, F32), pltpu.VMEM((2, SHOTS, STRIDE, Z), F32), dma((PARTS,))],
    )[1]


def after(value, *others):
    return lax.optimization_barrier((value, *others))[0]


def shards(right_side, wavenumber_sq, source_cell, source_amplitude):
    shots = right_side.shape[1]
    raw = right_side.reshape(2, shots, B * B, Z)
    k2 = wavenumber_sq[0]
    args = (raw, k2, source_cell, source_amplitude)
    xs = [swap(*pair_of(faces(start, *args), X0, X1)) for start in (0, SHOTS)]
    us, vs, es, cbs, ws, cws = zip(*[inner(start, *args) for start in (0, SHOTS)])
    xs[0] = after(xs[0], us[1])
    ys = [swap(*pair_of(y_faces(n * SHOTS, *xs[n], us[n], k2), Y0, Y1)) for n in range(2)]
    w = ws[0]
    exs, gs = [], []
    es = list(es)
    cwh = weights(*xs[0], *ys[0], k2)
    for n in range(2):
        u, v, es[n], w, *ex = ring(n * SHOTS, *xs[n], *ys[n], cbs[n], cws[0], us[n], vs[n], es[n], w)
        exs.append(swap(*pair_of(ex, X0, X1)))
        gs.append((u, v))
    gs = [base(*g, w) for g in gs]
    exs[0] = after(exs[0], *gs)
    eys = []
    for n in range(2):
        es[n], *ey = coarse_y(*exs[n], es[n])
        eys.append(swap(*pair_of(ey, Y0, Y1)))
    out = None
    for n in range(2):
        out = final(n * SHOTS, *eys[n], cwh, w, gs[n], es[n], out)
    return out.reshape(right_side.shape)


def pair_of(values, first_pairs, second_pairs):
    first, second = values
    return first, first_pairs, second, second_pairs


def solution(mesh):
    return jax.shard_map(
        shards,
        mesh=mesh,
        in_specs=(
            P(None, "shot", "space", None, None, None),
            P("space", None, None, None),
            P("shot"),
            P(None, "shot"),
        ),
        out_specs=P(None, "shot", "space", None, None, None),
        check_vma=False,
    )
```

time: 183 us -> 82.9 us (0.45)
  other arithmetic: 62.6 us -> 0 us
  starting transfers between devices: 83.3 us -> 47.2 us
  Pallas kernels: 0 us -> 26.3 us
  waiting for transfers between devices: 26.2 us -> 8.53 us
  local copies, waits for them, and re-layouts: 9.31 us -> 0.01 us
    ppermute x24 -> x16, starting transfers between devices: 83.3 us -> 47.2 us  [the longest x8 41.1 us: swap(): second = lax.ppermute(second, 'space', second_pairs)]
    add x18 -> x0, other arithmetic: 31.6 us -> none  [the longest x6 19.3 us: tile_operator(): near = weight_x * (along_x + along_y) + along_z]
    pallas_call x0 -> x15, Pallas kernels: none -> 26.3 us  [call(): pl.pallas_call(kernel, in_specs=[pl.BlockSpec(memory_space=spaces[kind])...]
    ppermute x24 -> x16, waiting for transfers between devices: 26.2 us -> 8.53 us  [the longest x8 8.51 us: swap(): second = lax.ppermute(second, 'space', second_pairs)]
    mul x12 -> x0, other arithmetic: 11.5 us -> none  [the longest x4 4.48 us: shards(): hit_x[:, :, None, None] * hit_y[:, None, :, None] * hit_z[:, None, None, :]]
    broadcast_in_dim x2 -> x0, local copies, waits for them, and re-layouts: 6.66 us -> none  [refine(): return jnp.repeat(jnp.repeat(field, 2, axis=-3), 2, axis=-2)]
    another operation x16 -> x0, other arithmetic: 6.25 us -> none  [relax(): return jnp.stack([real, imag])]
    sub x3 -> x0, other arithmetic: 6.02 us -> none  [the longest x1 5.13 us: shards(): rest = rhs - tile_operator(field, fine_faces(field), fine_r, fine_i, 1.0)]
  transfers between devices with their start and end apart: 24 -> 16, of which waited for: 10 -> 3; matrix products, arithmetic and copies ran while one was open for 7% -> 0% of each run, Pallas kernels for 0% -> 25%
where the time goes in v1:
time: 82.9 us; the launch traced here: 82.5 us
  starting transfers between devices  47.2 us (57%)
  Pallas kernels  26.3 us (32%)
  waiting for transfers between devices  8.53 us (10%)
    ppermute x8, starting transfers between devices, swap(): second = lax.ppermute(second, 'space', second_pairs)  41.1 us
    pallas_call x15, Pallas kernels, call(): pl.pallas_call(kernel, in_specs=[pl.BlockSpec(memory_space=spaces[kind])...  26.3 us
    ppermute x8, waiting for transfers between devices, swap(): second = lax.ppermute(second, 'space', second_pairs)  8.51 us
    ppermute x8, starting transfers between devices, swap(): first = lax.ppermute(first, 'space', first_pairs)  6.1 us
  transfers between devices with their start and end apart: 16, of which 3 were waited for; matrix products, arithmetic and copies ran while one was open for 0% of the time, Pallas kernels for 25%

profile of v1, /device:TPU:69, one launch (start us, length us, event | category | flops | bytes accessed | tf_op | source)
XLA Modules:
  0.0 82.5 jit_solution(12338573384307412888)
XLA Ops:
  0.0 1.3 %shard_map.50 = (f32[552,128]{1,0:T(8,128)S(1)}, f32[552,128]{1,0:T(8,128)S(1)}) custom-call(s32[16]{0:T(128)} %cell_in.7, f32[2,16]{1,0:T(2,128)} %amp_in.7, f32[2,16,256,128]{3,2,1,0:T(8,128)} %bitcast.12, f32[16,16,128]{2,1,0:T(8,128)} %bitcast.5), custom_call_target="tpu_custom_call" | custom-call | flops 1 | bytes 1 | tf_op jit(solution)/shard_map/pallas_call | solution.py:418
  1.4 7.3 %collective-permute-start.5 = (f32[552,128]{1,0:T(8,128)S(1)}, f32[552,128]{1,0:T(8,128)S(1)}, u32[]{:S(2)}, u32[]{:S(2)}) collective-permute-start(f32[552,128]{1,0:T(8,128)S(1)} %get-tuple-element.57), channel_id=1, source_target_pairs={{4,8},{8,4},{5,9},{9,5},{6,10},{10,6},{7,11},{11,7},{20,24},{24,20... | collective-permute-start | bytes 847880 | tf_op jit(solution)/shard_map/ppermute | solution.py:442
  8.7 1.3 %shard_map.46 = (f32[512,128]{1,0:T(8,128)S(1)}, f32[512,128]{1,0:T(8,128)S(1)}) custom-call(s32[16]{0:T(128)} %cell_in.7, f32[2,16]{1,0:T(2,128)} %amp_in.7, f32[2,16,256,128]{3,2,1,0:T(8,128)} %bitcast.13, f32[16,16,128]{2,1,0:T(8,128)} %bitcast.6), custom_call_target="tpu_custom_call" | custom-call | flops 1 | bytes 1 | tf_op jit(solution)/shard_map/pallas_call | solution.py:418
  10.1 1.9 %collective-permute-start.1 = (f32[512,128]{1,0:T(8,128)S(1)}, f32[512,128]{1,0:T(8,128)S(1)}, u32[]{:S(2)}, u32[]{:S(2)}) collective-permute-start(f32[512,128]{1,0:T(8,128)S(1)} %get-tuple-element.48), channel_id=1, source_target_pairs={{4,8},{8,4},{5,9},{9,5},{6,10},{10,6},{7,11},{11,7},{20,24},{24,20... | collective-permute-start | bytes 786440 | tf_op jit(solution)/shard_map/ppermute | solution.py:442
  12.0 3.5 %shard_map.49 = (f32[2,20,20,8,128]{4,3,2,1,0:T(8,128)S(1)}, f32[2,18,18,8,128]{4,3,2,1,0:T(8,128)S(1)}, f32[2,16,16,8,128]{4,3,2,1,0:T(8,128)S(1)}, f32[2,8,8,8...) custom-call(s32[16]{0:T(128)} %cell_in.7, f32[2,16]{1,0:T(2,128)} %amp_in.7, ...), custom_call_target="tpu_custom_call" | custom-call | flops 1 | bytes 1 | tf_op jit(solution)/shard_map/pallas_call | solution.py:418
  15.6 4.2 %shard_map.47 = (f32[2,20,20,8,128]{4,3,2,1,0:T(8,128)S(1)}, f32[2,18,18,8,128]{4,3,2,1,0:T(8,128)S(1)}, f32[2,16,16,8,128]{4,3,2,1,0:T(8,128)S(1)}, f32[2,8,8,8...) custom-call(s32[16]{0:T(128)} %cell_in.7, f32[2,16]{1,0:T(2,128)} %amp_in.7, ...), custom_call_target="tpu_custom_call" | custom-call | flops 1 | bytes 1 | tf_op jit(solution)/shard_map/pallas_call | solution.py:418
  19.8 5.7 %collective-permute-done.5.x1_ref = f32[552,128]{1,0:T(8,128)S(1)} collective-permute-done((f32[552,128]{1,0:T(8,128)S(1)}, f32[552,128]{1,0:T(8,128)S(1)}, u32[]{:S(2)}, u32[]{:S(2)}) %collective-permute-start.5) | collective-permute-done | bytes 282656 | tf_op jit(solution)/shard_map/ppermute | solution.py:442
  25.6 2.8 %collective-permute-start.6 = (f32[608,128]{1,0:T(8,128)S(1)}, f32[608,128]{1,0:T(8,128)S(1)}, u32[]{:S(2)}, u32[]{:S(2)}) collective-permute-start(f32[608,128]{1,0:T(8,128)S(1)} %get-tuple-element.61), channel_id=1, source_target_pairs={{0,1},{1,0},{2,3},{3,2},{4,5},{5,4},{6,7},{7,6},{8,9},{9,8},{10,11... | collective-permute-start | bytes 933896 | tf_op jit(solution)/shard_map/ppermute | solution.py:441
  28.4 1.9 %collective-permute-start.7 = (f32[608,128]{1,0:T(8,128)S(1)}, f32[608,128]{1,0:T(8,128)S(1)}, u32[]{:S(2)}, u32[]{:S(2)}) collective-permute-start(f32[608,128]{1,0:T(8,128)S(1)} %get-tuple-element.62), channel_id=1, source_target_pairs={{1,2},{2,1},{5,6},{6,5},{9,10},{10,9},{13,14},{14,13},{17,18},{18,... | collective-permute-start | bytes 933896 | tf_op jit(solution)/shard_map/ppermute | solution.py:442
  30.3 1.0 %collective-permute-done.1.x1_ref = f32[512,128]{1,0:T(8,128)S(1)} collective-permute-done((f32[512,128]{1,0:T(8,128)S(1)}, f32[512,128]{1,0:T(8,128)S(1)}, u32[]{:S(2)}, u32[]{:S(2)}) %collective-permute-start.1) | collective-permute-done | bytes 262176 | tf_op jit(solution)/shard_map/ppermute | solution.py:442
  31.4 2.7 %collective-permute-start.2 = (f32[544,128]{1,0:T(8,128)S(1)}, f32[544,128]{1,0:T(8,128)S(1)}, u32[]{:S(2)}, u32[]{:S(2)}) collective-permute-start(f32[544,128]{1,0:T(8,128)S(1)} %get-tuple-element.50), channel_id=1, source_target_pairs={{0,1},{1,0},{2,3},{3,2},{4,5},{5,4},{6,7},{7,6},{8,9},{9,8},{10,11... | collective-permute-start | bytes 835592 | tf_op jit(solution)/shard_map/ppermute | solution.py:441
  34.1 2.5 %collective-permute-start.3 = (f32[544,128]{1,0:T(8,128)S(1)}, f32[544,128]{1,0:T(8,128)S(1)}, u32[]{:S(2)}, u32[]{:S(2)}) collective-permute-start(f32[544,128]{1,0:T(8,128)S(1)} %get-tuple-element.51), channel_id=1, source_target_pairs={{1,2},{2,1},{5,6},{6,5},{9,10},{10,9},{13,14},{14,13},{17,18},{18,... | collective-permute-start | bytes 835592 | tf_op jit(solution)/shard_map/ppermute | solution.py:442
  36.7 1.7 %shard_map.52 = (f32[2,20,20,8,128]{4,3,2,1,0:T(8,128)S(1)}, f32[2,18,18,8,128]{4,3,2,1,0:T(8,128)S(1)}, f32[2,16,16,8,128]{4,3,2,1,0:T(8,128)S(1)}, f32[2,18,18...) custom-call(f32[552,128]{1,0:T(8,128)S(1)} %collective-permute-done., ...), custom_call_target="tpu_custom_call", output_to_operand_aliasing={{0}: (6, {}), {1}: (7, {}), {2}: (8, {}), {3}: (9, {})} | custom-call | flops 1 | bytes 1 | tf_op jit(solution)/shard_map/pallas_call | solution.py:418
  38.5 6.3 %collective-permute-start.13 = (f32[512,128]{1,0:T(8,128)S(1)}, f32[512,128]{1,0:T(8,128)S(1)}, u32[]{:S(2)}, u32[]{:S(2)}) collective-permute-start(f32[512,128]{1,0:T(8,128)S(1)} %get-tuple-element.78), channel_id=1, source_target_pairs={{4,8},{8,4},{5,9},{9,5},{6,10},{10,6},{7,11},{11,7},{20,24},{24,20... | collective-permute-start | bytes 786440 | tf_op jit(solution)/shard_map/ppermute | solution.py:442
  44.8 1.7 %shard_map.53 = (f32[2,20,20,8,128]{4,3,2,1,0:T(8,128)S(1)}, f32[2,18,18,8,128]{4,3,2,1,0:T(8,128)S(1)}, f32[2,16,16,8,128]{4,3,2,1,0:T(8,128)S(1)}, f32[2,18,18...) custom-call(f32[512,128]{1,0:T(8,128)S(1)} %collective-permute-done., ...), custom_call_target="tpu_custom_call", output_to_operand_aliasing={{0}: (6, {}), {1}: (7, {}), {2}: (8, {}), {3}: (9, {})} | custom-call | flops 1 | bytes 1 | tf_op jit(solution)/shard_map/pallas_call | solution.py:418
  46.6 8.7 %collective-permute-start.9 = (f32[512,128]{1,0:T(8,128)S(1)}, f32[512,128]{1,0:T(8,128)S(1)}, u32[]{:S(2)}, u32[]{:S(2)}) collective-permute-start(f32[512,128]{1,0:T(8,128)S(1)} %get-tuple-element.69), channel_id=1, source_target_pairs={{4,8},{8,4},{5,9},{9,5},{6,10},{10,6},{7,11},{11,7},{20,24},{24,20... | collective-permute-start | bytes 786440 | tf_op jit(solution)/shard_map/ppermute | solution.py:442
  55.3 1.7 %shard_map.57.g_ref = f32[2,16,16,8,128]{4,3,2,1,0:T(8,128)S(1)} custom-call(f32[2,20,20,8,128]{4,3,2,1,0:T(8,128)S(1)} %get-tuple-element.79.u_ref, f32[2,18,18,8,128]{4,3,2,1,0:T(8,128)S(1)} %get-tuple-element.80.v_ref, f32[2,18,18,128]{3,2,1,0:T(8,128)S(1)} %get-tuple-element.73.w_ref), custom_call_target="tpu_custom_call" | custom-call | flops 1 | bytes 1 | tf_op jit(solution)/shard_map/pallas_call | solution.py:418
  57.0 1.7 %shard_map.56.g_ref = f32[2,16,16,8,128]{4,3,2,1,0:T(8,128)S(1)} custom-call(f32[2,20,20,8,128]{4,3,2,1,0:T(8,128)S(1)} %get-tuple-element.74.u_ref, f32[2,18,18,8,128]{4,3,2,1,0:T(8,128)S(1)} %get-tuple-element.75.v_ref, f32[2,18,18,128]{3,2,1,0:T(8,128)S(1)} %get-tuple-element.73.w_ref), custom_call_target="tpu_custom_call" | custom-call | flops 1 | bytes 1 | tf_op jit(solution)/shard_map/pallas_call | solution.py:418
  58.7 0.1 shard_map.58
  59.0 9.6 %collective-permute-start.15 = (f32[704,128]{1,0:T(8,128)S(1)}, f32[704,128]{1,0:T(8,128)S(1)}, u32[]{:S(2)}, u32[]{:S(2)}) collective-permute-start(f32[704,128]{1,0:T(8,128)S(1)} %get-tuple-element.85), channel_id=1, source_target_pairs={{1,2},{2,1},{5,6},{6,5},{9,10},{10,9},{13,14},{14,13},{17,18},{18,... | collective-permute-start | bytes 1081352 | tf_op jit(solution)/shard_map/ppermute | solution.py:442
  68.9 2.9 %collective-permute-start.11 = (f32[704,128]{1,0:T(8,128)S(1)}, f32[704,128]{1,0:T(8,128)S(1)}, u32[]{:S(2)}, u32[]{:S(2)}) collective-permute-start(f32[704,128]{1,0:T(8,128)S(1)} %get-tuple-element.72), channel_id=1, source_target_pairs={{1,2},{2,1},{5,6},{6,5},{9,10},{10,9},{13,14},{14,13},{17,18},{18,... | collective-permute-start | bytes 1081352 | tf_op jit(solution)/shard_map/ppermute | solution.py:442
  71.9 1.8 %collective-permute-done.15.ey1_ref = f32[704,128]{1,0:T(8,128)S(1)} collective-permute-done((f32[704,128]{1,0:T(8,128)S(1)}, f32[704,128]{1,0:T(8,128)S(1)}, u32[]{:S(2)}, u32[]{:S(2)}) %collective-permute-start.15) | collective-permute-done | bytes 360480 | tf_op jit(solution)/shard_map/ppermute | solution.py:442
  73.7 4.3 %shard_map.59 = (f32[2,16,16,8,128]{4,3,2,1,0:T(8,128)S(1)}, f32[2,16,256,128]{3,2,1,0:T(8,128)}) custom-call(f32[704,128]{1,0:T(8,128)S(1)} %collective-permute-done.14.ey0_ref, f32[704,128]{1,0:T(8,128)S(1)} %collective-permute-done.15.ey1_ref, f32[2,14,14,128]{3,2,1,0:T(8,128)S(1)} %shard_map.55.cwh_ref, ...), custom_call_target="tpu_custom_call", output_to_operand_aliasing={{0}: (5, {})} | custom-call | flops 1 | bytes 1 | tf_op jit(solution)/shard_map/pallas_call | solution.py:418
  78.0 4.3 %shard_map.60 = (f32[2,16,16,8,128]{4,3,2,1,0:T(8,128)S(1)}, f32[2,16,256,128]{3,2,1,0:T(8,128)}) custom-call(f32[704,128]{1,0:T(8,128)S(1)} %collective-permute-done.10.ey0_ref, f32[704,128]{1,0:T(8,128)S(1)} %collective-permute-done.11.ey1_ref, f32[2,14,14,128]{3,2,1,0:T(8,128)S(1)} %shard_map.55.cwh_ref, ...), custom_call_target="tpu_custom_call", output_to_operand_aliasing={{0}: (5, {}), {1}: (6, {})} | custom-call | flops 1 | bytes 1 | tf_op jit(solution)/shard_map/pallas_call | solution.py:418
  (25 shorter events, 1.0 us)
Async XLA Ops:
  1.3 18.5 %collective-permute-start.4 = (f32[552,128]{1,0:T(8,128)S(1)}, f32[552,128]{1,0:T(8,128)S(1)}, u32[]{:S(2)}, u32[]{:S(2)}) collective-permute-start(f32[552,128]{1,0:T(8,128)S(1)} %get-tuple-element.56), channel_id=1, source_target_pairs={{0,4},{4,0},{1,5},{5,1},{2,6},{6,2},{3,7},{7,3},{8,12},{12,8},{9,1... | collective-permute-start | bytes 847880 | tf_op jit(solution)/shard_map/ppermute | solution.py:441
  1.4 24.0 %collective-permute-start.5 = (f32[552,128]{1,0:T(8,128)S(1)}, f32[552,128]{1,0:T(8,128)S(1)}, u32[]{:S(2)}, u32[]{:S(2)}) collective-permute-start(f32[552,128]{1,0:T(8,128)S(1)} %get-tuple-element.57), channel_id=1, source_target_pairs={{4,8},{8,4},{5,9},{9,5},{6,10},{10,6},{7,11},{11,7},{20,24},{24,20... | collective-permute-start | bytes 847880 | tf_op jit(solution)/shard_map/ppermute | solution.py:442
  10.0 20.3 %collective-permute-start = (f32[512,128]{1,0:T(8,128)S(1)}, f32[512,128]{1,0:T(8,128)S(1)}, u32[]{:S(2)}, u32[]{:S(2)}) collective-permute-start(f32[512,128]{1,0:T(8,128)S(1)} %get-tuple-element.47), channel_id=1, source_target_pairs={{0,4},{4,0},{1,5},{5,1},{2,6},{6,2},{3,7},{7,3},{8,12},{12,8},{9,1... | collective-permute-start | bytes 786440 | tf_op jit(solution)/shard_map/ppermute | solution.py:441
  10.1 21.3 %collective-permute-start.1 = (f32[512,128]{1,0:T(8,128)S(1)}, f32[512,128]{1,0:T(8,128)S(1)}, u32[]{:S(2)}, u32[]{:S(2)}) collective-permute-start(f32[512,128]{1,0:T(8,128)S(1)} %get-tuple-element.48), channel_id=1, source_target_pairs={{4,8},{8,4},{5,9},{9,5},{6,10},{10,6},{7,11},{11,7},{20,24},{24,20... | collective-permute-start | bytes 786440 | tf_op jit(solution)/shard_map/ppermute | solution.py:442
  15.5 9.9 %copy-start = (f32[1,16,16,128]{3,2,1,0:T(8,128)S(1)}, f32[1,16,16,128]{3,2,1,0:T(8,128)}, u32[]{:S(2)}) copy-start(f32[1,16,16,128]{3,2,1,0:T(8,128)} %param.5) | copy-start | bytes 393220
  25.6 11.1 %collective-permute-start.6 = (f32[608,128]{1,0:T(8,128)S(1)}, f32[608,128]{1,0:T(8,128)S(1)}, u32[]{:S(2)}, u32[]{:S(2)}) collective-permute-start(f32[608,128]{1,0:T(8,128)S(1)} %get-tuple-element.61), channel_id=1, source_target_pairs={{0,1},{1,0},{2,3},{3,2},{4,5},{5,4},{6,7},{7,6},{8,9},{9,8},{10,11... | collective-permute-start | bytes 933896 | tf_op jit(solution)/shard_map/ppermute | solution.py:441
  28.4 8.3 %collective-permute-start.7 = (f32[608,128]{1,0:T(8,128)S(1)}, f32[608,128]{1,0:T(8,128)S(1)}, u32[]{:S(2)}, u32[]{:S(2)}) collective-permute-start(f32[608,128]{1,0:T(8,128)S(1)} %get-tuple-element.62), channel_id=1, source_target_pairs={{1,2},{2,1},{5,6},{6,5},{9,10},{10,9},{13,14},{14,13},{17,18},{18,... | collective-permute-start | bytes 933896 | tf_op jit(solution)/shard_map/ppermute | solution.py:442
  31.4 13.4 %collective-permute-start.2 = (f32[544,128]{1,0:T(8,128)S(1)}, f32[544,128]{1,0:T(8,128)S(1)}, u32[]{:S(2)}, u32[]{:S(2)}) collective-permute-start(f32[544,128]{1,0:T(8,128)S(1)} %get-tuple-element.50), channel_id=1, source_target_pairs={{0,1},{1,0},{2,3},{3,2},{4,5},{5,4},{6,7},{7,6},{8,9},{9,8},{10,11... | collective-permute-start | bytes 835592 | tf_op jit(solution)/shard_map/ppermute | solution.py:441
  34.1 10.7 %collective-permute-start.3 = (f32[544,128]{1,0:T(8,128)S(1)}, f32[544,128]{1,0:T(8,128)S(1)}, u32[]{:S(2)}, u32[]{:S(2)}) collective-permute-start(f32[544,128]{1,0:T(8,128)S(1)} %get-tuple-element.51), channel_id=1, source_target_pairs={{1,2},{2,1},{5,6},{6,5},{9,10},{10,9},{13,14},{14,13},{17,18},{18,... | collective-permute-start | bytes 835592 | tf_op jit(solution)/shard_map/ppermute | solution.py:442
  38.4 20.3 %collective-permute-start.12 = (f32[512,128]{1,0:T(8,128)S(1)}, f32[512,128]{1,0:T(8,128)S(1)}, u32[]{:S(2)}, u32[]{:S(2)}) collective-permute-start(f32[512,128]{1,0:T(8,128)S(1)} %get-tuple-element.77), channel_id=1, source_target_pairs={{0,4},{4,0},{1,5},{5,1},{2,6},{6,2},{3,7},{7,3},{8,12},{12,8},{9,1... | collective-permute-start | bytes 786440 | tf_op jit(solution)/shard_map/ppermute | solution.py:441
  38.5 20.2 %collective-permute-start.13 = (f32[512,128]{1,0:T(8,128)S(1)}, f32[512,128]{1,0:T(8,128)S(1)}, u32[]{:S(2)}, u32[]{:S(2)}) collective-permute-start(f32[512,128]{1,0:T(8,128)S(1)} %get-tuple-element.78), channel_id=1, source_target_pairs={{4,8},{8,4},{5,9},{9,5},{6,10},{10,6},{7,11},{11,7},{20,24},{24,20... | collective-permute-start | bytes 786440 | tf_op jit(solution)/shard_map/ppermute | solution.py:442
  46.5 22.0 %collective-permute-start.8 = (f32[512,128]{1,0:T(8,128)S(1)}, f32[512,128]{1,0:T(8,128)S(1)}, u32[]{:S(2)}, u32[]{:S(2)}) collective-permute-start(f32[512,128]{1,0:T(8,128)S(1)} %get-tuple-element.68), channel_id=1, source_target_pairs={{0,4},{4,0},{1,5},{5,1},{2,6},{6,2},{3,7},{7,3},{8,12},{12,8},{9,1... | collective-permute-start | bytes 786440 | tf_op jit(solution)/shard_map/ppermute | solution.py:441
  46.6 21.9 %collective-permute-start.9 = (f32[512,128]{1,0:T(8,128)S(1)}, f32[512,128]{1,0:T(8,128)S(1)}, u32[]{:S(2)}, u32[]{:S(2)}) collective-permute-start(f32[512,128]{1,0:T(8,128)S(1)} %get-tuple-element.69), channel_id=1, source_target_pairs={{4,8},{8,4},{5,9},{9,5},{6,10},{10,6},{7,11},{11,7},{20,24},{24,20... | collective-permute-start | bytes 786440 | tf_op jit(solution)/shard_map/ppermute | solution.py:442
  58.9 13.0 %collective-permute-start.14 = (f32[704,128]{1,0:T(8,128)S(1)}, f32[704,128]{1,0:T(8,128)S(1)}, u32[]{:S(2)}, u32[]{:S(2)}) collective-permute-start(f32[704,128]{1,0:T(8,128)S(1)} %get-tuple-element.84), channel_id=1, source_target_pairs={{0,1},{1,0},{2,3},{3,2},{4,5},{5,4},{6,7},{7,6},{8,9},{9,8},{10,11... | collective-permute-start | bytes 1081352 | tf_op jit(solution)/shard_map/ppermute | solution.py:441
  59.0 14.7 %collective-permute-start.15 = (f32[704,128]{1,0:T(8,128)S(1)}, f32[704,128]{1,0:T(8,128)S(1)}, u32[]{:S(2)}, u32[]{:S(2)}) collective-permute-start(f32[704,128]{1,0:T(8,128)S(1)} %get-tuple-element.85), channel_id=1, source_target_pairs={{1,2},{2,1},{5,6},{6,5},{9,10},{10,9},{13,14},{14,13},{17,18},{18,... | collective-permute-start | bytes 1081352 | tf_op jit(solution)/shard_map/ppermute | solution.py:442
  68.8 9.2 %collective-permute-start.10 = (f32[704,128]{1,0:T(8,128)S(1)}, f32[704,128]{1,0:T(8,128)S(1)}, u32[]{:S(2)}, u32[]{:S(2)}) collective-permute-start(f32[704,128]{1,0:T(8,128)S(1)} %get-tuple-element.71), channel_id=1, source_target_pairs={{0,1},{1,0},{2,3},{3,2},{4,5},{5,4},{6,7},{7,6},{8,9},{9,8},{10,11... | collective-permute-start | bytes 1081352 | tf_op jit(solution)/shard_map/ppermute | solution.py:441
  68.9 9.2 %collective-permute-start.11 = (f32[704,128]{1,0:T(8,128)S(1)}, f32[704,128]{1,0:T(8,128)S(1)}, u32[]{:S(2)}, u32[]{:S(2)}) collective-permute-start(f32[704,128]{1,0:T(8,128)S(1)} %get-tuple-element.72), channel_id=1, source_target_pairs={{1,2},{2,1},{5,6},{6,5},{9,10},{10,9},{13,14},{14,13},{17,18},{18,... | collective-permute-start | bytes 1081352 | tf_op jit(solution)/shard_map/ppermute | solution.py:442

commit v2 on v1

--- a/solution.py
+++ b/solution.py
@@ -14,7 +14,7 @@
 C = 8
 Z = 128
 F32 = jnp.float32
-UNROLL = 4
+UNROLL = 8
 PARTS = 2
 FACE_STRIDE = 2 * B + 8
 STRIDE = B * B + 8
@@ -209,7 +209,7 @@
         first_coarse(shots, v_ref, cb_ref, cw_ref, e_ref, [(x, y) for y in range(1, C - 1)])
 
 
-def y_faces_kernel(start, shots, x0_ref, x1_ref, u_ref, k2_ref, y0_ref, y1_ref):
+def y_faces_kernel(start, shots, x1_ref, x0_ref, u_ref, k2_ref, y0_ref, y1_ref):
     row, column = place()
     even = row % 2 == 0
     flag = column % 2
@@ -244,7 +244,7 @@
             out[pl.ds(at + 14, 2), :] = jnp.zeros((2, Z), F32)
 
 
-def ring_kernel(start, shots, x0_ref, x1_ref, y0_ref, y1_ref, cb_ref, cw_ref, u_in, v_in, e_in, w_in, u_ref, v_ref, e_ref, w_ref, ex0_ref, ex1_ref):
+def ring_kernel(start, shots, y1_ref, y0_ref, x1_ref, x0_ref, cb_ref, cw_ref, u_in, v_in, e_in, w_in, u_ref, v_ref, e_ref, w_ref, ex0_ref, ex1_ref):
     del u_in, v_in, e_in, w_in
     row, column = place()
     flag_x, flag_y = row % 2, column % 2
@@ -275,15 +275,15 @@
             w_ref[0, x + 1, pl.ds(to, 1), :] = w_r[x : x + 1]
             w_ref[1, x + 1, pl.ds(to, 1), :] = w_i[x : x + 1]
 
-    @pl.loop(0, B, unroll=UNROLL)
+    @pl.loop(0, B, unroll=4)
     def _(y):
         second_v(shots, u_ref, w_ref, v_ref, [(x, y) for x in (-1, 0, B - 1, B)])
 
-    @pl.loop(0, B, unroll=UNROLL)
+    @pl.loop(0, B, unroll=4)
     def _(x):
         second_v(shots, u_ref, w_ref, v_ref, [(x, y) for y in (-1, 0, B - 1, B)])
 
-    @pl.loop(0, C, unroll=UNROLL)
+    @pl.loop(0, C, unroll=4)
     def _(y):
         first_coarse(shots, v_ref, cb_ref, cw_ref, e_ref, [(x, y) for x in (0, C - 1)])
 
@@ -331,7 +331,7 @@
             g_ref[1, x, y] = v_ref[1, x + 1, y + 1] + 0.84 * u_ref[1, x + 2, y + 2] + i
 
 
-def coarse_y_kernel(shots, ex0_ref, ex1_ref, e_in, e_ref, ey0_ref, ey1_ref):
+def coarse_y_kernel(shots, ex1_ref, ex0_ref, e_in, e_ref, ey0_ref, ey1_ref):
     del e_in
     row, column = place()
     flag_x, flag_y = row % 2, column % 2
@@ -349,8 +349,33 @@
                     out[pl.ds(((Y_START[d] + n) * 2 + c) * shots, shots), :] = e_ref[c, 1 + d + n, y]
 
 
-def final_kernel(start, shots, ey0_ref, ey1_ref, cwh_ref, w_ref, g_ref, *refs):
-    e_ref, out_ref, e2_ref, e3_ref, stage_ref, sems = refs[-6:]
+def sweep(shots, cwh_ref, e_ref, old, new, x, cells):
+    along = [z_sum(old[c, x + 4, y + 4]) for y in cells for c in range(2)]
+    for n, y in enumerate(cells):
+        parts = []
+        for c in range(2):
+            sides = (old[c, x + 3, y + 4] + old[c, x + 5, y + 4]) + (old[c, x + 4, y + 3] + old[c, x + 4, y + 5])
+            parts.append(0.25 * sides + along[2 * n + c])
+        parts = times(*[row_of(cwh_ref, c, x + 3, y + 3, shots) for c in range(2)], *parts)
+        for c in range(2):
+            new[c, x + 4, y + 4] = 0.2 * old[c, x + 4, y + 4] + e_ref[c, x + 4, y + 4] + parts[c]
+
+
+def early_kernel(shots, cwh_ref, e_ref, e2_ref, e3_ref, e4_ref):
+    for n, (old, new) in enumerate(((e_ref, e2_ref), (e2_ref, e3_ref), (e3_ref, e4_ref))):
+        reach = 3 - n
+
+        @pl.loop(-reach, C + reach, unroll=C // 2 + reach)
+        def _(x, old=old, new=new, cells=range(n + 1, C - 1 - n)):
+            sweep(shots, cwh_ref, e_ref, old, new, x, cells)
+
+
+def final_kernel(start, shots, early, ey1_ref, ey0_ref, cwh_ref, w_ref, g_ref, *refs):
+    if early:
+        e_ref, out_ref, e2_ref, e3_ref, e4_ref, stage_ref, sems = refs[-7:]
+    else:
+        e_ref, out_ref, e2_ref, e3_ref, stage_ref, sems = refs[-6:]
+        e4_ref = e2_ref
     row, column = place()
     flag_y = column % 2
     for message, high in ((ey0_ref, flag_y == 0), (ey1_ref, flag_y == 1)):
@@ -361,35 +386,27 @@
                     e_ref[c, 1 + d + n, to] = message[pl.ds(((Y_START[d] + n) * 2 + c) * shots, shots), :]
     stage = stage_ref.reshape(2, shots * STRIDE, Z)
 
-    def sweep(old, new, x, reach_y):
-        cells = range(-reach_y, C + reach_y)
-        along = [z_sum(old[c, x + 4, y + 4]) for y in cells for c in range(2)]
-        for n, y in enumerate(cells):
-            parts = []
-            for c in range(2):
-                sides = (old[c, x + 3, y + 4] + old[c, x + 5, y + 4]) + (old[c, x + 4, y + 3] + old[c, x + 4, y + 5])
-                parts.append(0.25 * sides + along[2 * n + c])
-            w_r, w_i = row_of(cwh_ref, 0, x + 3, y + 3, shots), row_of(cwh_ref, 1, x + 3, y + 3, shots)
-            parts = times(w_r, w_i, *parts)
-            for c in range(2):
-                new[c, x + 4, y + 4] = 0.2 * old[c, x + 4, y + 4] + e_ref[c, x + 4, y + 4] + parts[c]
-
-    for old, new, reach in ((e_ref, e2_ref, 3), (e2_ref, e3_ref, 2), (e3_ref, e2_ref, 1)):
+    for n, (old, new) in enumerate(((e_ref, e2_ref), (e2_ref, e3_ref), (e3_ref, e4_ref))):
+        reach = 3 - n
+
+        def cells(extent):
+            every = range(-extent, C + extent)
+            return [y for y in every if not (early and n < y < C - 1 - n)]
 
         @pl.loop(0, C, unroll=UNROLL)
-        def _(x, old=old, new=new, reach=reach):
-            sweep(old, new, x, reach)
+        def _(x, old=old, new=new):
+            sweep(shots, cwh_ref, e_ref, old, new, x, cells(reach))
 
         for d in range(1, reach + 1):
             for x in (-d, C - 1 + d):
-                sweep(old, new, x, reach - d)
+                sweep(shots, cwh_ref, e_ref, old, new, x, cells(reach - d))
 
     def finish(x):
-        along = [z_sum(e2_ref[c, x + 4, y + 4]) for y in range(C) for c in range(2)]
+        along = [z_sum(e4_ref[c, x + 4, y + 4]) for y in range(C) for c in range(2)]
         for y in range(C):
-            e = [e2_ref[c, x + 4, y + 4] for c in range(2)]
-            near_x = [[e2_ref[c, x + 3 + 2 * half, y + 4] for c in range(2)] for half in range(2)]
-            near_y = [[e2_ref[c, x + 4, y + 3 + 2 * half] for c in range(2)] for half in range(2)]
+            e = [e4_ref[c, x + 4, y + 4] for c in range(2)]
+            near_x = [[e4_ref[c, x + 3 + 2 * half, y + 4] for c in range(2)] for half in range(2)]
+            near_y = [[e4_ref[c, x + 4, y + 3 + 2 * half] for c in range(2)] for half in range(2)]
             middle = [2.0 * e[c] + along[2 * y + c] for c in range(2)]
             for half in range(2):
                 total = [middle[c] + near_x[half][c] for c in range(2)]
@@ -477,13 +494,13 @@
 def y_faces(start, x0, x1, u, k2):
     return call(
         part(y_faces_kernel, start, SHOTS),
-        [("r", x0), ("r", x1), ("r", u), ("r", k2)],
+        [("r", x1), ("r", x0), ("r", u), ("r", k2)],
         [(68 * SHOTS + (0 if start else 64), Z)] * 2,
     )
 
 
 def ring(start, x0, x1, y0, y1, cb, cw, u, v, e, w):
-    inputs = [("r", value) for value in (x0, x1, y0, y1, cb, cw, u, v, e, w)]
+    inputs = [("r", value) for value in (y1, y0, x1, x0, cb, cw, u, v, e, w)]
     return call(
         part(ring_kernel, start, SHOTS),
         inputs,
@@ -504,22 +521,30 @@
 def coarse_y(ex0, ex1, e):
     return call(
         part(coarse_y_kernel, SHOTS),
-        [("r", ex0), ("r", ex1), ("r", e)],
+        [("r", ex1), ("r", ex0), ("r", e)],
         [E_SHAPE, (88 * SHOTS, Z), (88 * SHOTS, Z)],
         aliases={2: 0},
     )
 
 
-def final(start, ey0, ey1, cwh, w, g, e, out):
+def early_sweeps(cwh, e):
+    return call(part(early_kernel, SHOTS), [("r", cwh), ("r", e)], [E_SHAPE] * 3)
+
+
+def final(start, ey0, ey1, cwh, w, g, e, out, early=()):
     total = 2 * SHOTS
-    inputs = [("r", value) for value in (ey0, ey1, cwh, w, g, e)] + ([] if out is None else [("h", out)])
+    inputs = [("r", value) for value in (ey1, ey0, cwh, w, g, e)] + ([] if out is None else [("h", out)])
+    aliases = {5: 0} if out is None else {5: 0, 6: 1}
+    for n, value in enumerate(early):
+        aliases[len(inputs)] = 2 + n
+        inputs.append(("r", value))
     return call(
-        part(final_kernel, start, SHOTS),
+        part(final_kernel, start, SHOTS, len(early) > 0),
         inputs,
-        [E_SHAPE, (2, total, B * B, Z)],
-        aliases={5: 0} if out is None else {5: 0, 6: 1},
+        [E_SHAPE, (2, total, B * B, Z)] + [E_SHAPE] * len(early),
+        aliases=aliases,
         out_any=(1,),
-        scratch=[pltpu.VMEM(E_SHAPE, F32), pltpu.VMEM(E_SHAPE, F32), pltpu.VMEM((2, SHOTS, STRIDE, Z), F32), dma((PARTS,))],
+        scratch=[pltpu.VMEM(E_SHAPE, F32)] * (0 if early else 2) + [pltpu.VMEM((2, SHOTS, STRIDE, Z), F32), dma((PARTS,))],
     )[1]
 
 
@@ -550,9 +575,11 @@
     for n in range(2):
         es[n], *ey = coarse_y(*exs[n], es[n])
         eys.append(swap(*pair_of(ey, Y0, Y1)))
-    out = None
-    for n in range(2):
-        out = final(n * SHOTS, *eys[n], cwh, w, gs[n], es[n], out)
+        if n == 0:
+            early = early_sweeps(cwh, es[0])
+            es[1] = after(es[1], *early)
+    out = final(0, *eys[0], cwh, w, gs[0], es[0], None, early)
+    out = final(SHOTS, *eys[1], cwh, w, gs[1], es[1], out)
     return out.reshape(right_side.shape)
 
 

time: 82.9 us -> 80.4 us (0.970)
  starting transfers between devices: 47.2 us -> 28.1 us
  waiting for transfers between devices: 8.53 us -> 25.4 us
    ppermute x8, waiting for transfers between devices: 8.51 us -> 25.1 us  [swap(): second = lax.ppermute(second, 'space', second_pairs)]
    ppermute x8, starting transfers between devices: 41.1 us -> 26.5 us  [swap(): second = lax.ppermute(second, 'space', second_pairs)]
    ppermute x8, starting transfers between devices: 6.1 us -> 1.61 us  [swap(): first = lax.ppermute(first, 'space', first_pairs)]
    pallas_call x15 -> x16, Pallas kernels: 26.3 us -> 26 us  [call(): pl.pallas_call(kernel, in_specs=[pl.BlockSpec(memory_space=spaces[kind])...]
  transfers between devices with their start and end apart: 16 -> 16, of which waited for: 3 -> 7; matrix products, arithmetic and copies ran while one was open for 0% -> 0% of each run, Pallas kernels for 25% -> 26%
where the time goes in v2:
time: 80.4 us; the launch traced here: 80 us
  starting transfers between devices  28.1 us (35%)
  Pallas kernels  26 us (32%)
  waiting for transfers between devices  25.4 us (32%)
    ppermute x8, starting transfers between devices, swap(): second = lax.ppermute(second, 'space', second_pairs)  26.5 us
    pallas_call x16, Pallas kernels, call(): pl.pallas_call(kernel, in_specs=[pl.BlockSpec(memory_space=spaces[kind])...  26 us
    ppermute x8, waiting for transfers between devices, swap(): second = lax.ppermute(second, 'space', second_pairs)  25.1 us
  transfers between devices with their start and end apart: 16, of which 7 were waited for; matrix products, arithmetic and copies ran while one was open for 0% of the time, Pallas kernels for 26%

profile of v2, /device:TPU:69, one launch (start us, length us, event | category | flops | bytes accessed | tf_op | source)
XLA Modules:
  0.0 80.0 jit_solution(13441093468447456115)
XLA Ops:
  0.0 1.3 %shard_map.50 = (f32[552,128]{1,0:T(8,128)S(1)}, f32[552,128]{1,0:T(8,128)S(1)}) custom-call(s32[16]{0:T(128)} %cell_in.7, f32[2,16]{1,0:T(2,128)} %amp_in.7, f32[2,16,256,128]{3,2,1,0:T(8,128)} %bitcast.12, f32[16,16,128]{2,1,0:T(8,128)} %bitcast.5), custom_call_target="tpu_custom_call" | custom-call | flops 1 | bytes 1 | tf_op jit(solution)/shard_map/pallas_call | solution.py:435
  1.4 7.3 %collective-permute-start.5 = (f32[552,128]{1,0:T(8,128)S(1)}, f32[552,128]{1,0:T(8,128)S(1)}, u32[]{:S(2)}, u32[]{:S(2)}) collective-permute-start(f32[552,128]{1,0:T(8,128)S(1)} %get-tuple-element.61), channel_id=1, source_target_pairs={{4,8},{8,4},{5,9},{9,5},{6,10},{10,6},{7,11},{11,7},{20,24},{24,20... | collective-permute-start | bytes 847880 | tf_op jit(solution)/shard_map/ppermute | solution.py:459
  8.7 1.3 %shard_map.46 = (f32[512,128]{1,0:T(8,128)S(1)}, f32[512,128]{1,0:T(8,128)S(1)}) custom-call(s32[16]{0:T(128)} %cell_in.7, f32[2,16]{1,0:T(2,128)} %amp_in.7, f32[2,16,256,128]{3,2,1,0:T(8,128)} %bitcast.13, f32[16,16,128]{2,1,0:T(8,128)} %bitcast.6), custom_call_target="tpu_custom_call" | custom-call | flops 1 | bytes 1 | tf_op jit(solution)/shard_map/pallas_call | solution.py:435
  10.0 1.9 %collective-permute-start = (f32[512,128]{1,0:T(8,128)S(1)}, f32[512,128]{1,0:T(8,128)S(1)}, u32[]{:S(2)}, u32[]{:S(2)}) collective-permute-start(f32[512,128]{1,0:T(8,128)S(1)} %get-tuple-element.51), channel_id=1, source_target_pairs={{4,8},{8,4},{5,9},{9,5},{6,10},{10,6},{7,11},{11,7},{20,24},{24,20... | collective-permute-start | bytes 786440 | tf_op jit(solution)/shard_map/ppermute | solution.py:459
  12.0 4.2 %shard_map.47 = (f32[2,20,20,8,128]{4,3,2,1,0:T(8,128)S(1)}, f32[2,18,18,8,128]{4,3,2,1,0:T(8,128)S(1)}, f32[2,16,16,8,128]{4,3,2,1,0:T(8,128)S(1)}, f32[2,8,8,8...) custom-call(s32[16]{0:T(128)} %cell_in.7, f32[2,16]{1,0:T(2,128)} %amp_in.7, ...), custom_call_target="tpu_custom_call" | custom-call | flops 1 | bytes 1 | tf_op jit(solution)/shard_map/pallas_call | solution.py:435
  16.2 3.5 %shard_map.49 = (f32[2,20,20,8,128]{4,3,2,1,0:T(8,128)S(1)}, f32[2,18,18,8,128]{4,3,2,1,0:T(8,128)S(1)}, f32[2,16,16,8,128]{4,3,2,1,0:T(8,128)S(1)}, f32[2,8,8,8...) custom-call(s32[16]{0:T(128)} %cell_in.7, f32[2,16]{1,0:T(2,128)} %amp_in.7, ...), custom_call_target="tpu_custom_call" | custom-call | flops 1 | bytes 1 | tf_op jit(solution)/shard_map/pallas_call | solution.py:435
  19.7 6.5 %collective-permute-done.5.x1_ref = f32[552,128]{1,0:T(8,128)S(1)} collective-permute-done((f32[552,128]{1,0:T(8,128)S(1)}, f32[552,128]{1,0:T(8,128)S(1)}, u32[]{:S(2)}, u32[]{:S(2)}) %collective-permute-start.5) | collective-permute-done | bytes 282656 | tf_op jit(solution)/shard_map/ppermute | solution.py:459
  26.4 1.9 %collective-permute-start.6 = (f32[608,128]{1,0:T(8,128)S(1)}, f32[608,128]{1,0:T(8,128)S(1)}, u32[]{:S(2)}, u32[]{:S(2)}) collective-permute-start(f32[608,128]{1,0:T(8,128)S(1)} %get-tuple-element.65), channel_id=1, source_target_pairs={{1,2},{2,1},{5,6},{6,5},{9,10},{10,9},{13,14},{14,13},{17,18},{18,... | collective-permute-start | bytes 933896 | tf_op jit(solution)/shard_map/ppermute | solution.py:459
  29.1 2.8 %collective-permute-done.x1_ref = f32[512,128]{1,0:T(8,128)S(1)} collective-permute-done((f32[512,128]{1,0:T(8,128)S(1)}, f32[512,128]{1,0:T(8,128)S(1)}, u32[]{:S(2)}, u32[]{:S(2)}) %collective-permute-start) | collective-permute-done | bytes 262176 | tf_op jit(solution)/shard_map/ppermute | solution.py:459
  32.0 3.9 %collective-permute-start.2 = (f32[544,128]{1,0:T(8,128)S(1)}, f32[544,128]{1,0:T(8,128)S(1)}, u32[]{:S(2)}, u32[]{:S(2)}) collective-permute-start(f32[544,128]{1,0:T(8,128)S(1)} %get-tuple-element.54), channel_id=1, source_target_pairs={{1,2},{2,1},{5,6},{6,5},{9,10},{10,9},{13,14},{14,13},{17,18},{18,... | collective-permute-start | bytes 835592 | tf_op jit(solution)/shard_map/ppermute | solution.py:459
  36.0 1.7 %shard_map.52 = (f32[2,20,20,8,128]{4,3,2,1,0:T(8,128)S(1)}, f32[2,18,18,8,128]{4,3,2,1,0:T(8,128)S(1)}, f32[2,16,16,8,128]{4,3,2,1,0:T(8,128)S(1)}, f32[2,18,18...) custom-call(f32[608,128]{1,0:T(8,128)S(1)} %collective-permute-done., ...), custom_call_target="tpu_custom_call", output_to_operand_aliasing={{0}: (6, {}), {1}: (7, {}), {2}: (8, {}), {3}: (9, {})} | custom-call | flops 1 | bytes 1 | tf_op jit(solution)/shard_map/pallas_call | solution.py:435
  37.8 5.0 %collective-permute-start.11 = (f32[512,128]{1,0:T(8,128)S(1)}, f32[512,128]{1,0:T(8,128)S(1)}, u32[]{:S(2)}, u32[]{:S(2)}) collective-permute-start(f32[512,128]{1,0:T(8,128)S(1)} %get-tuple-element.76), channel_id=1, source_target_pairs={{4,8},{8,4},{5,9},{9,5},{6,10},{10,6},{7,11},{11,7},{20,24},{24,20... | collective-permute-start | bytes 786440 | tf_op jit(solution)/shard_map/ppermute | solution.py:459
  42.9 1.7 %shard_map.53 = (f32[2,20,20,8,128]{4,3,2,1,0:T(8,128)S(1)}, f32[2,18,18,8,128]{4,3,2,1,0:T(8,128)S(1)}, f32[2,16,16,8,128]{4,3,2,1,0:T(8,128)S(1)}, f32[2,18,18...) custom-call(f32[544,128]{1,0:T(8,128)S(1)} %collective-permute-done., ...), custom_call_target="tpu_custom_call", output_to_operand_aliasing={{0}: (6, {}), {1}: (7, {}), {2}: (8, {}), {3}: (9, {})} | custom-call | flops 1 | bytes 1 | tf_op jit(solution)/shard_map/pallas_call | solution.py:435
  44.6 2.6 %collective-permute-start.8 = (f32[512,128]{1,0:T(8,128)S(1)}, f32[512,128]{1,0:T(8,128)S(1)}, u32[]{:S(2)}, u32[]{:S(2)}) collective-permute-start(f32[512,128]{1,0:T(8,128)S(1)} %get-tuple-element.72), channel_id=1, source_target_pairs={{4,8},{8,4},{5,9},{9,5},{6,10},{10,6},{7,11},{11,7},{20,24},{24,20... | collective-permute-start | bytes 786440 | tf_op jit(solution)/shard_map/ppermute | solution.py:459
  47.3 1.7 %shard_map.56.g_ref = f32[2,16,16,8,128]{4,3,2,1,0:T(8,128)S(1)} custom-call(f32[2,20,20,8,128]{4,3,2,1,0:T(8,128)S(1)} %get-tuple-element.80.u_ref, f32[2,18,18,8,128]{4,3,2,1,0:T(8,128)S(1)} %get-tuple-element.81.v_ref, f32[2,18,18,128]{3,2,1,0:T(8,128)S(1)} %get-tuple-element.79.w_ref), custom_call_target="tpu_custom_call" | custom-call | flops 1 | bytes 1 | tf_op jit(solution)/shard_map/pallas_call | solution.py:435
  49.0 1.7 %shard_map.55.g_ref = f32[2,16,16,8,128]{4,3,2,1,0:T(8,128)S(1)} custom-call(f32[2,20,20,8,128]{4,3,2,1,0:T(8,128)S(1)} %get-tuple-element.77.u_ref, f32[2,18,18,8,128]{4,3,2,1,0:T(8,128)S(1)} %get-tuple-element.78.v_ref, f32[2,18,18,128]{3,2,1,0:T(8,128)S(1)} %get-tuple-element.79.w_ref), custom_call_target="tpu_custom_call" | custom-call | flops 1 | bytes 1 | tf_op jit(solution)/shard_map/pallas_call | solution.py:435
  51.1 10.1 %collective-permute-done.11.ex1_ref = f32[512,128]{1,0:T(8,128)S(1)} collective-permute-done((f32[512,128]{1,0:T(8,128)S(1)}, f32[512,128]{1,0:T(8,128)S(1)}, u32[]{:S(2)}, u32[]{:S(2)}) %collective-permute-start.11) | collective-permute-done | bytes 262176 | tf_op jit(solution)/shard_map/ppermute | solution.py:459
  62.5 1.9 %collective-permute-start.14 = (f32[704,128]{1,0:T(8,128)S(1)}, f32[704,128]{1,0:T(8,128)S(1)}, u32[]{:S(2)}, u32[]{:S(2)}) collective-permute-start(f32[704,128]{1,0:T(8,128)S(1)} %get-tuple-element.93), channel_id=1, source_target_pairs={{1,2},{2,1},{5,6},{6,5},{9,10},{10,9},{13,14},{14,13},{17,18},{18,... | collective-permute-start | bytes 1081352 | tf_op jit(solution)/shard_map/ppermute | solution.py:459
  64.5 2.3 %collective-permute-done.8.ex1_ref = f32[512,128]{1,0:T(8,128)S(1)} collective-permute-done((f32[512,128]{1,0:T(8,128)S(1)}, f32[512,128]{1,0:T(8,128)S(1)}, u32[]{:S(2)}, u32[]{:S(2)}) %collective-permute-start.8) | collective-permute-done | bytes 262176 | tf_op jit(solution)/shard_map/ppermute | solution.py:459
  67.0 1.9 %collective-permute-start.12 = (f32[704,128]{1,0:T(8,128)S(1)}, f32[704,128]{1,0:T(8,128)S(1)}, u32[]{:S(2)}, u32[]{:S(2)}) collective-permute-start(f32[704,128]{1,0:T(8,128)S(1)} %get-tuple-element.90), channel_id=1, source_target_pairs={{1,2},{2,1},{5,6},{6,5},{9,10},{10,9},{13,14},{14,13},{17,18},{18,... | collective-permute-start | bytes 1081352 | tf_op jit(solution)/shard_map/ppermute | solution.py:459
  69.2 2.0 %collective-permute-done.14.ey1_ref = f32[704,128]{1,0:T(8,128)S(1)} collective-permute-done((f32[704,128]{1,0:T(8,128)S(1)}, f32[704,128]{1,0:T(8,128)S(1)}, u32[]{:S(2)}, u32[]{:S(2)}) %collective-permute-start.14) | collective-permute-done | bytes 360480 | tf_op jit(solution)/shard_map/ppermute | solution.py:459
  71.2 3.2 %shard_map.60 = (f32[2,16,16,8,128]{4,3,2,1,0:T(8,128)S(1)}, f32[2,16,256,128]{3,2,1,0:T(8,128)}, f32[2,16,16,8,128]{4,3,2,1,0:T(8,128)S(1)}, f32[2,16,16,8,128]...) custom-call(f32[704,128]{1,0:T(8,128)S(1)} %collective-permute-done., ...), custom_call_target="tpu_custom_call", output_to_operand_aliasing={{0}: (5, {}), {2}: (6, {}), {3}: (7, {}), {4}: (8, {})} | custom-call | flops 1 | bytes 1 | tf_op jit(solution)/shard_map/pallas_call | solution.py:435
  74.4 1.3 %collective-permute-done.12.ey1_ref = f32[704,128]{1,0:T(8,128)S(1)} collective-permute-done((f32[704,128]{1,0:T(8,128)S(1)}, f32[704,128]{1,0:T(8,128)S(1)}, u32[]{:S(2)}, u32[]{:S(2)}) %collective-permute-start.12) | collective-permute-done | bytes 360480 | tf_op jit(solution)/shard_map/ppermute | solution.py:459
  75.8 4.1 %shard_map.61 = (f32[2,16,16,8,128]{4,3,2,1,0:T(8,128)S(1)}, f32[2,16,256,128]{3,2,1,0:T(8,128)}) custom-call(f32[704,128]{1,0:T(8,128)S(1)} %collective-permute-done.12.ey1_ref, f32[704,128]{1,0:T(8,128)S(1)} %collective-permute-done.13.ey0_ref, f32[2,14,14,128]{3,2,1,0:T(8,128)S(1)} %shard_map.54.cwh_ref, ...), custom_call_target="tpu_custom_call", output_to_operand_aliasing={{0}: (5, {}), {1}: (6, {})} | custom-call | flops 1 | bytes 1 | tf_op jit(solution)/shard_map/pallas_call | solution.py:435
  (26 shorter events, 3.6 us)
Async XLA Ops:
  1.3 18.4 %collective-permute-start.4 = (f32[552,128]{1,0:T(8,128)S(1)}, f32[552,128]{1,0:T(8,128)S(1)}, u32[]{:S(2)}, u32[]{:S(2)}) collective-permute-start(f32[552,128]{1,0:T(8,128)S(1)} %get-tuple-element.60), channel_id=1, source_target_pairs={{0,4},{4,0},{1,5},{5,1},{2,6},{6,2},{3,7},{7,3},{8,12},{12,8},{9,1... | collective-permute-start | bytes 847880 | tf_op jit(solution)/shard_map/ppermute | solution.py:458
  1.4 24.9 %collective-permute-start.5 = (f32[552,128]{1,0:T(8,128)S(1)}, f32[552,128]{1,0:T(8,128)S(1)}, u32[]{:S(2)}, u32[]{:S(2)}) collective-permute-start(f32[552,128]{1,0:T(8,128)S(1)} %get-tuple-element.61), channel_id=1, source_target_pairs={{4,8},{8,4},{5,9},{9,5},{6,10},{10,6},{7,11},{11,7},{20,24},{24,20... | collective-permute-start | bytes 847880 | tf_op jit(solution)/shard_map/ppermute | solution.py:459
  10.0 21.9 %collective-permute-start = (f32[512,128]{1,0:T(8,128)S(1)}, f32[512,128]{1,0:T(8,128)S(1)}, u32[]{:S(2)}, u32[]{:S(2)}) collective-permute-start(f32[512,128]{1,0:T(8,128)S(1)} %get-tuple-element.51), channel_id=1, source_target_pairs={{4,8},{8,4},{5,9},{9,5},{6,10},{10,6},{7,11},{11,7},{20,24},{24,20... | collective-permute-start | bytes 786440 | tf_op jit(solution)/shard_map/ppermute | solution.py:459
  11.9 20.0 %collective-permute-start.1 = (f32[512,128]{1,0:T(8,128)S(1)}, f32[512,128]{1,0:T(8,128)S(1)}, u32[]{:S(2)}, u32[]{:S(2)}) collective-permute-start(f32[512,128]{1,0:T(8,128)S(1)} %get-tuple-element.52), channel_id=1, source_target_pairs={{0,4},{4,0},{1,5},{5,1},{2,6},{6,2},{3,7},{7,3},{8,12},{12,8},{9,1... | collective-permute-start | bytes 786440 | tf_op jit(solution)/shard_map/ppermute | solution.py:458
  16.2 10.1 %copy-start = (f32[1,16,16,128]{3,2,1,0:T(8,128)S(1)}, f32[1,16,16,128]{3,2,1,0:T(8,128)}, u32[]{:S(2)}) copy-start(f32[1,16,16,128]{3,2,1,0:T(8,128)} %param.5) | copy-start | bytes 393220
  26.4 9.6 %collective-permute-start.6 = (f32[608,128]{1,0:T(8,128)S(1)}, f32[608,128]{1,0:T(8,128)S(1)}, u32[]{:S(2)}, u32[]{:S(2)}) collective-permute-start(f32[608,128]{1,0:T(8,128)S(1)} %get-tuple-element.65), channel_id=1, source_target_pairs={{1,2},{2,1},{5,6},{6,5},{9,10},{10,9},{13,14},{14,13},{17,18},{18,... | collective-permute-start | bytes 933896 | tf_op jit(solution)/shard_map/ppermute | solution.py:459
  28.3 7.7 %collective-permute-start.7 = (f32[608,128]{1,0:T(8,128)S(1)}, f32[608,128]{1,0:T(8,128)S(1)}, u32[]{:S(2)}, u32[]{:S(2)}) collective-permute-start(f32[608,128]{1,0:T(8,128)S(1)} %get-tuple-element.66), channel_id=1, source_target_pairs={{0,1},{1,0},{2,3},{3,2},{4,5},{5,4},{6,7},{7,6},{8,9},{9,8},{10,11... | collective-permute-start | bytes 933896 | tf_op jit(solution)/shard_map/ppermute | solution.py:458
  32.0 10.9 %collective-permute-start.2 = (f32[544,128]{1,0:T(8,128)S(1)}, f32[544,128]{1,0:T(8,128)S(1)}, u32[]{:S(2)}, u32[]{:S(2)}) collective-permute-start(f32[544,128]{1,0:T(8,128)S(1)} %get-tuple-element.54), channel_id=1, source_target_pairs={{1,2},{2,1},{5,6},{6,5},{9,10},{10,9},{13,14},{14,13},{17,18},{18,... | collective-permute-start | bytes 835592 | tf_op jit(solution)/shard_map/ppermute | solution.py:459
  35.9 7.0 %collective-permute-start.3 = (f32[544,128]{1,0:T(8,128)S(1)}, f32[544,128]{1,0:T(8,128)S(1)}, u32[]{:S(2)}, u32[]{:S(2)}) collective-permute-start(f32[544,128]{1,0:T(8,128)S(1)} %get-tuple-element.55), channel_id=1, source_target_pairs={{0,1},{1,0},{2,3},{3,2},{4,5},{5,4},{6,7},{7,6},{8,9},{9,8},{10,11... | collective-permute-start | bytes 835592 | tf_op jit(solution)/shard_map/ppermute | solution.py:458
  37.7 13.4 %collective-permute-start.10 = (f32[512,128]{1,0:T(8,128)S(1)}, f32[512,128]{1,0:T(8,128)S(1)}, u32[]{:S(2)}, u32[]{:S(2)}) collective-permute-start(f32[512,128]{1,0:T(8,128)S(1)} %get-tuple-element.75), channel_id=1, source_target_pairs={{0,4},{4,0},{1,5},{5,1},{2,6},{6,2},{3,7},{7,3},{8,12},{12,8},{9,1... | collective-permute-start | bytes 786440 | tf_op jit(solution)/shard_map/ppermute | solution.py:458
  37.8 23.4 %collective-permute-start.11 = (f32[512,128]{1,0:T(8,128)S(1)}, f32[512,128]{1,0:T(8,128)S(1)}, u32[]{:S(2)}, u32[]{:S(2)}) collective-permute-start(f32[512,128]{1,0:T(8,128)S(1)} %get-tuple-element.76), channel_id=1, source_target_pairs={{4,8},{8,4},{5,9},{9,5},{6,10},{10,6},{7,11},{11,7},{20,24},{24,20... | collective-permute-start | bytes 786440 | tf_op jit(solution)/shard_map/ppermute | solution.py:459
  44.6 22.2 %collective-permute-start.8 = (f32[512,128]{1,0:T(8,128)S(1)}, f32[512,128]{1,0:T(8,128)S(1)}, u32[]{:S(2)}, u32[]{:S(2)}) collective-permute-start(f32[512,128]{1,0:T(8,128)S(1)} %get-tuple-element.72), channel_id=1, source_target_pairs={{4,8},{8,4},{5,9},{9,5},{6,10},{10,6},{7,11},{11,7},{20,24},{24,20... | collective-permute-start | bytes 786440 | tf_op jit(solution)/shard_map/ppermute | solution.py:459
  47.2 19.6 %collective-permute-start.9 = (f32[512,128]{1,0:T(8,128)S(1)}, f32[512,128]{1,0:T(8,128)S(1)}, u32[]{:S(2)}, u32[]{:S(2)}) collective-permute-start(f32[512,128]{1,0:T(8,128)S(1)} %get-tuple-element.73), channel_id=1, source_target_pairs={{0,4},{4,0},{1,5},{5,1},{2,6},{6,2},{3,7},{7,3},{8,12},{12,8},{9,1... | collective-permute-start | bytes 786440 | tf_op jit(solution)/shard_map/ppermute | solution.py:458
  62.5 8.7 %collective-permute-start.14 = (f32[704,128]{1,0:T(8,128)S(1)}, f32[704,128]{1,0:T(8,128)S(1)}, u32[]{:S(2)}, u32[]{:S(2)}) collective-permute-start(f32[704,128]{1,0:T(8,128)S(1)} %get-tuple-element.93), channel_id=1, source_target_pairs={{1,2},{2,1},{5,6},{6,5},{9,10},{10,9},{13,14},{14,13},{17,18},{18,... | collective-permute-start | bytes 1081352 | tf_op jit(solution)/shard_map/ppermute | solution.py:459
  64.4 6.8 %collective-permute-start.15 = (f32[704,128]{1,0:T(8,128)S(1)}, f32[704,128]{1,0:T(8,128)S(1)}, u32[]{:S(2)}, u32[]{:S(2)}) collective-permute-start(f32[704,128]{1,0:T(8,128)S(1)} %get-tuple-element.94), channel_id=1, source_target_pairs={{0,1},{1,0},{2,3},{3,2},{4,5},{5,4},{6,7},{7,6},{8,9},{9,8},{10,11... | collective-permute-start | bytes 1081352 | tf_op jit(solution)/shard_map/ppermute | solution.py:458
  67.0 8.7 %collective-permute-start.12 = (f32[704,128]{1,0:T(8,128)S(1)}, f32[704,128]{1,0:T(8,128)S(1)}, u32[]{:S(2)}, u32[]{:S(2)}) collective-permute-start(f32[704,128]{1,0:T(8,128)S(1)} %get-tuple-element.90), channel_id=1, source_target_pairs={{1,2},{2,1},{5,6},{6,5},{9,10},{10,9},{13,14},{14,13},{17,18},{18,... | collective-permute-start | bytes 1081352 | tf_op jit(solution)/shard_map/ppermute | solution.py:459
  68.9 6.8 %collective-permute-start.13 = (f32[704,128]{1,0:T(8,128)S(1)}, f32[704,128]{1,0:T(8,128)S(1)}, u32[]{:S(2)}, u32[]{:S(2)}) collective-permute-start(f32[704,128]{1,0:T(8,128)S(1)} %get-tuple-element.91), channel_id=1, source_target_pairs={{0,1},{1,0},{2,3},{3,2},{4,5},{5,4},{6,7},{7,6},{8,9},{9,8},{10,11... | collective-permute-start | bytes 1081352 | tf_op jit(solution)/shard_map/ppermute | solution.py:458

commit v3 on v2

--- a/solution.py
+++ b/solution.py
@@ -15,7 +15,7 @@
 Z = 128
 F32 = jnp.float32
 UNROLL = 8
-PARTS = 2
+PARTS = 4
 FACE_STRIDE = 2 * B + 8
 STRIDE = B * B + 8
 Y_COUNT = (14, 12, 10, 8)
@@ -571,15 +571,16 @@
         gs.append((u, v))
     gs = [base(*g, w) for g in gs]
     exs[0] = after(exs[0], *gs)
-    eys = []
+    eys, early = [], []
     for n in range(2):
         es[n], *ey = coarse_y(*exs[n], es[n])
         eys.append(swap(*pair_of(ey, Y0, Y1)))
+        early.append(early_sweeps(cwh, es[n]))
         if n == 0:
-            early = early_sweeps(cwh, es[0])
-            es[1] = after(es[1], *early)
-    out = final(0, *eys[0], cwh, w, gs[0], es[0], None, early)
-    out = final(SHOTS, *eys[1], cwh, w, gs[1], es[1], out)
+            es[1] = after(es[1], *early[0])
+    eys[0] = after(eys[0][::-1], *early[1])[::-1]
+    out = final(0, *eys[0], cwh, w, gs[0], es[0], None, early[0])
+    out = final(SHOTS, *eys[1], cwh, w, gs[1], es[1], out, early[1])
     return out.reshape(right_side.shape)
 
 

time: 80.4 us -> 79.4 us (0.988)
  waiting for transfers between devices: 25.4 us -> 24.3 us
    ppermute x8, waiting for transfers between devices: 25.1 us -> 24 us  [swap(): second = lax.ppermute(second, 'space', second_pairs)]
    pallas_call x16 -> x17, Pallas kernels: 26 us -> 26.1 us  [call(): pl.pallas_call(kernel, in_specs=[pl.BlockSpec(memory_space=spaces[kind])...]
  transfers between devices with their start and end apart: 16 -> 16, of which waited for: 7 -> 7; matrix products, arithmetic and copies ran while one was open for 0% -> 0% of each run, Pallas kernels for 26% -> 27%
where the time goes in v3:
time: 79.4 us; the launch traced here: 79.1 us
  starting transfers between devices  28.1 us (35%)
  Pallas kernels  26.1 us (33%)
  waiting for transfers between devices  24.3 us (31%)
    ppermute x8, starting transfers between devices, swap(): second = lax.ppermute(second, 'space', second_pairs)  26.5 us
    pallas_call x17, Pallas kernels, call(): pl.pallas_call(kernel, in_specs=[pl.BlockSpec(memory_space=spaces[kind])...  26.1 us
    ppermute x8, waiting for transfers between devices, swap(): second = lax.ppermute(second, 'space', second_pairs)  24 us
    ppermute x8, starting transfers between devices, swap(): first = lax.ppermute(first, 'space', first_pairs)  1.61 us
  transfers between devices with their start and end apart: 16, of which 7 were waited for; matrix products, arithmetic and copies ran while one was open for 0% of the time, Pallas kernels for 27%

profile of v3, /device:TPU:69, one launch (start us, length us, event | category | flops | bytes accessed | tf_op | source)
XLA Modules:
  0.0 79.1 jit_solution(2413283037027048392)
XLA Ops:
  0.0 1.3 %shard_map.50 = (f32[552,128]{1,0:T(8,128)S(1)}, f32[552,128]{1,0:T(8,128)S(1)}) custom-call(s32[16]{0:T(128)} %cell_in.7, f32[2,16]{1,0:T(2,128)} %amp_in.7, f32[2,16,256,128]{3,2,1,0:T(8,128)} %bitcast.12, f32[16,16,128]{2,1,0:T(8,128)} %bitcast.5), custom_call_target="tpu_custom_call" | custom-call | flops 1 | bytes 1 | tf_op jit(solution)/shard_map/pallas_call | solution.py:435
  1.4 7.3 %collective-permute-start.5 = (f32[552,128]{1,0:T(8,128)S(1)}, f32[552,128]{1,0:T(8,128)S(1)}, u32[]{:S(2)}, u32[]{:S(2)}) collective-permute-start(f32[552,128]{1,0:T(8,128)S(1)} %get-tuple-element.66), channel_id=1, source_target_pairs={{4,8},{8,4},{5,9},{9,5},{6,10},{10,6},{7,11},{11,7},{20,24},{24,20... | collective-permute-start | bytes 847880 | tf_op jit(solution)/shard_map/ppermute | solution.py:459
  8.7 1.3 %shard_map.46 = (f32[512,128]{1,0:T(8,128)S(1)}, f32[512,128]{1,0:T(8,128)S(1)}) custom-call(s32[16]{0:T(128)} %cell_in.7, f32[2,16]{1,0:T(2,128)} %amp_in.7, f32[2,16,256,128]{3,2,1,0:T(8,128)} %bitcast.13, f32[16,16,128]{2,1,0:T(8,128)} %bitcast.6), custom_call_target="tpu_custom_call" | custom-call | flops 1 | bytes 1 | tf_op jit(solution)/shard_map/pallas_call | solution.py:435
  10.0 1.9 %collective-permute-start = (f32[512,128]{1,0:T(8,128)S(1)}, f32[512,128]{1,0:T(8,128)S(1)}, u32[]{:S(2)}, u32[]{:S(2)}) collective-permute-start(f32[512,128]{1,0:T(8,128)S(1)} %get-tuple-element.56), channel_id=1, source_target_pairs={{4,8},{8,4},{5,9},{9,5},{6,10},{10,6},{7,11},{11,7},{20,24},{24,20... | collective-permute-start | bytes 786440 | tf_op jit(solution)/shard_map/ppermute | solution.py:459
  12.0 3.5 %shard_map.49 = (f32[2,20,20,8,128]{4,3,2,1,0:T(8,128)S(1)}, f32[2,18,18,8,128]{4,3,2,1,0:T(8,128)S(1)}, f32[2,16,16,8,128]{4,3,2,1,0:T(8,128)S(1)}, f32[2,8,8,8...) custom-call(s32[16]{0:T(128)} %cell_in.7, f32[2,16]{1,0:T(2,128)} %amp_in.7, ...), custom_call_target="tpu_custom_call" | custom-call | flops 1 | bytes 1 | tf_op jit(solution)/shard_map/pallas_call | solution.py:435
  15.5 4.2 %shard_map.47 = (f32[2,20,20,8,128]{4,3,2,1,0:T(8,128)S(1)}, f32[2,18,18,8,128]{4,3,2,1,0:T(8,128)S(1)}, f32[2,16,16,8,128]{4,3,2,1,0:T(8,128)S(1)}, f32[2,8,8,8...) custom-call(s32[16]{0:T(128)} %cell_in.7, f32[2,16]{1,0:T(2,128)} %amp_in.7, ...), custom_call_target="tpu_custom_call" | custom-call | flops 1 | bytes 1 | tf_op jit(solution)/shard_map/pallas_call | solution.py:435
  19.7 6.5 %collective-permute-done.5.x1_ref = f32[552,128]{1,0:T(8,128)S(1)} collective-permute-done((f32[552,128]{1,0:T(8,128)S(1)}, f32[552,128]{1,0:T(8,128)S(1)}, u32[]{:S(2)}, u32[]{:S(2)}) %collective-permute-start.5) | collective-permute-done | bytes 282656 | tf_op jit(solution)/shard_map/ppermute | solution.py:459
  26.4 1.9 %collective-permute-start.6 = (f32[608,128]{1,0:T(8,128)S(1)}, f32[608,128]{1,0:T(8,128)S(1)}, u32[]{:S(2)}, u32[]{:S(2)}) collective-permute-start(f32[608,128]{1,0:T(8,128)S(1)} %get-tuple-element.70), channel_id=1, source_target_pairs={{1,2},{2,1},{5,6},{6,5},{9,10},{10,9},{13,14},{14,13},{17,18},{18,... | collective-permute-start | bytes 933896 | tf_op jit(solution)/shard_map/ppermute | solution.py:459
  29.1 2.8 %collective-permute-done.x1_ref = f32[512,128]{1,0:T(8,128)S(1)} collective-permute-done((f32[512,128]{1,0:T(8,128)S(1)}, f32[512,128]{1,0:T(8,128)S(1)}, u32[]{:S(2)}, u32[]{:S(2)}) %collective-permute-start) | collective-permute-done | bytes 262176 | tf_op jit(solution)/shard_map/ppermute | solution.py:459
  32.0 3.9 %collective-permute-start.2 = (f32[544,128]{1,0:T(8,128)S(1)}, f32[544,128]{1,0:T(8,128)S(1)}, u32[]{:S(2)}, u32[]{:S(2)}) collective-permute-start(f32[544,128]{1,0:T(8,128)S(1)} %get-tuple-element.59), channel_id=1, source_target_pairs={{1,2},{2,1},{5,6},{6,5},{9,10},{10,9},{13,14},{14,13},{17,18},{18,... | collective-permute-start | bytes 835592 | tf_op jit(solution)/shard_map/ppermute | solution.py:459
  36.0 1.7 %shard_map.52 = (f32[2,20,20,8,128]{4,3,2,1,0:T(8,128)S(1)}, f32[2,18,18,8,128]{4,3,2,1,0:T(8,128)S(1)}, f32[2,16,16,8,128]{4,3,2,1,0:T(8,128)S(1)}, f32[2,18,18...) custom-call(f32[608,128]{1,0:T(8,128)S(1)} %collective-permute-done., ...), custom_call_target="tpu_custom_call", output_to_operand_aliasing={{0}: (6, {}), {1}: (7, {}), {2}: (8, {}), {3}: (9, {})} | custom-call | flops 1 | bytes 1 | tf_op jit(solution)/shard_map/pallas_call | solution.py:435
  37.8 5.0 %collective-permute-start.11 = (f32[512,128]{1,0:T(8,128)S(1)}, f32[512,128]{1,0:T(8,128)S(1)}, u32[]{:S(2)}, u32[]{:S(2)}) collective-permute-start(f32[512,128]{1,0:T(8,128)S(1)} %get-tuple-element.81), channel_id=1, source_target_pairs={{4,8},{8,4},{5,9},{9,5},{6,10},{10,6},{7,11},{11,7},{20,24},{24,20... | collective-permute-start | bytes 786440 | tf_op jit(solution)/shard_map/ppermute | solution.py:459
  42.9 1.7 %shard_map.53 = (f32[2,20,20,8,128]{4,3,2,1,0:T(8,128)S(1)}, f32[2,18,18,8,128]{4,3,2,1,0:T(8,128)S(1)}, f32[2,16,16,8,128]{4,3,2,1,0:T(8,128)S(1)}, f32[2,18,18...) custom-call(f32[544,128]{1,0:T(8,128)S(1)} %collective-permute-done., ...), custom_call_target="tpu_custom_call", output_to_operand_aliasing={{0}: (6, {}), {1}: (7, {}), {2}: (8, {}), {3}: (9, {})} | custom-call | flops 1 | bytes 1 | tf_op jit(solution)/shard_map/pallas_call | solution.py:435
  44.6 2.6 %collective-permute-start.8 = (f32[512,128]{1,0:T(8,128)S(1)}, f32[512,128]{1,0:T(8,128)S(1)}, u32[]{:S(2)}, u32[]{:S(2)}) collective-permute-start(f32[512,128]{1,0:T(8,128)S(1)} %get-tuple-element.77), channel_id=1, source_target_pairs={{4,8},{8,4},{5,9},{9,5},{6,10},{10,6},{7,11},{11,7},{20,24},{24,20... | collective-permute-start | bytes 786440 | tf_op jit(solution)/shard_map/ppermute | solution.py:459
  47.3 1.7 %shard_map.55.g_ref = f32[2,16,16,8,128]{4,3,2,1,0:T(8,128)S(1)} custom-call(f32[2,20,20,8,128]{4,3,2,1,0:T(8,128)S(1)} %get-tuple-element.82.u_ref, f32[2,18,18,8,128]{4,3,2,1,0:T(8,128)S(1)} %get-tuple-element.83.v_ref, f32[2,18,18,128]{3,2,1,0:T(8,128)S(1)} %get-tuple-element.84.w_ref), custom_call_target="tpu_custom_call" | custom-call | flops 1 | bytes 1 | tf_op jit(solution)/shard_map/pallas_call | solution.py:435
  49.0 1.7 %shard_map.56.g_ref = f32[2,16,16,8,128]{4,3,2,1,0:T(8,128)S(1)} custom-call(f32[2,20,20,8,128]{4,3,2,1,0:T(8,128)S(1)} %get-tuple-element.85.u_ref, f32[2,18,18,8,128]{4,3,2,1,0:T(8,128)S(1)} %get-tuple-element.86.v_ref, f32[2,18,18,128]{3,2,1,0:T(8,128)S(1)} %get-tuple-element.84.w_ref), custom_call_target="tpu_custom_call" | custom-call | flops 1 | bytes 1 | tf_op jit(solution)/shard_map/pallas_call | solution.py:435
  51.1 10.1 %collective-permute-done.11.ex1_ref = f32[512,128]{1,0:T(8,128)S(1)} collective-permute-done((f32[512,128]{1,0:T(8,128)S(1)}, f32[512,128]{1,0:T(8,128)S(1)}, u32[]{:S(2)}, u32[]{:S(2)}) %collective-permute-start.11) | collective-permute-done | bytes 262176 | tf_op jit(solution)/shard_map/ppermute | solution.py:459
  61.4 1.9 %collective-permute-start.14 = (f32[704,128]{1,0:T(8,128)S(1)}, f32[704,128]{1,0:T(8,128)S(1)}, u32[]{:S(2)}, u32[]{:S(2)}) collective-permute-start(f32[704,128]{1,0:T(8,128)S(1)} %get-tuple-element.98), channel_id=1, source_target_pairs={{1,2},{2,1},{5,6},{6,5},{9,10},{10,9},{13,14},{14,13},{17,18},{18,... | collective-permute-start | bytes 1081352 | tf_op jit(solution)/shard_map/ppermute | solution.py:459
  64.5 2.3 %collective-permute-done.8.ex1_ref = f32[512,128]{1,0:T(8,128)S(1)} collective-permute-done((f32[512,128]{1,0:T(8,128)S(1)}, f32[512,128]{1,0:T(8,128)S(1)}, u32[]{:S(2)}, u32[]{:S(2)}) %collective-permute-start.8) | collective-permute-done | bytes 262176 | tf_op jit(solution)/shard_map/ppermute | solution.py:459
  67.0 1.9 %collective-permute-start.12 = (f32[704,128]{1,0:T(8,128)S(1)}, f32[704,128]{1,0:T(8,128)S(1)}, u32[]{:S(2)}, u32[]{:S(2)}) collective-permute-start(f32[704,128]{1,0:T(8,128)S(1)} %get-tuple-element.95), channel_id=1, source_target_pairs={{1,2},{2,1},{5,6},{6,5},{9,10},{10,9},{13,14},{14,13},{17,18},{18,... | collective-permute-start | bytes 1081352 | tf_op jit(solution)/shard_map/ppermute | solution.py:459
  69.2 1.1 %shard_map.60 = (f32[2,16,16,8,128]{4,3,2,1,0:T(8,128)S(1)}, f32[2,16,16,8,128]{4,3,2,1,0:T(8,128)S(1)}, f32[2,16,16,8,128]{4,3,2,1,0:T(8,128)S(1)}) custom-call(f32[2,14,14,128]{3,2,1,0:T(8,128)S(1)} %shard_map.54.cwh_ref, f32[2,16,16,8,128]{4,3,2,1,0:T(8,128)S(1)} %get-tuple-element.97.e_ref.refs_0_), custom_call_target="tpu_custom_call" | custom-call | flops 1 | bytes 1 | tf_op jit(solution)/shard_map/pallas_call | solution.py:435
  70.6 3.2 %shard_map.61 = (f32[2,16,16,8,128]{4,3,2,1,0:T(8,128)S(1)}, f32[2,16,256,128]{3,2,1,0:T(8,128)}, f32[2,16,16,8,128]{4,3,2,1,0:T(8,128)S(1)}, f32[2,16,16,8,128]...) custom-call(f32[704,128]{1,0:T(8,128)S(1)} %collective-permute-done., ...), custom_call_target="tpu_custom_call", output_to_operand_aliasing={{0}: (5, {}), {2}: (6, {}), {3}: (7, {}), {4}: (8, {})} | custom-call | flops 1 | bytes 1 | tf_op jit(solution)/shard_map/pallas_call | solution.py:435
  73.7 2.0 %collective-permute-done.12.ey1_ref = f32[704,128]{1,0:T(8,128)S(1)} collective-permute-done((f32[704,128]{1,0:T(8,128)S(1)}, f32[704,128]{1,0:T(8,128)S(1)}, u32[]{:S(2)}, u32[]{:S(2)}) %collective-permute-start.12) | collective-permute-done | bytes 360480 | tf_op jit(solution)/shard_map/ppermute | solution.py:459
  75.8 3.1 %shard_map.62 = (f32[2,16,16,8,128]{4,3,2,1,0:T(8,128)S(1)}, f32[2,16,256,128]{3,2,1,0:T(8,128)}, f32[2,16,16,8,128]{4,3,2,1,0:T(8,128)S(1)}, f32[2,16,16,8,128]...) custom-call(f32[704,128]{1,0:T(8,128)S(1)} %collective-permute-done., ...), custom_call_target="tpu_custom_call", output_to_operand_aliasing={{0}: (5, {}), {1}: (6, {}), {2}: (7, {}), {3}: (8, {}), {4}... | custom-call | flops 1 | bytes 1 | tf_op jit(solution)/shard_map/pallas_call | solution.py:435
  (27 shorter events, 3.8 us)
Async XLA Ops:
  1.3 18.4 %collective-permute-start.4 = (f32[552,128]{1,0:T(8,128)S(1)}, f32[552,128]{1,0:T(8,128)S(1)}, u32[]{:S(2)}, u32[]{:S(2)}) collective-permute-start(f32[552,128]{1,0:T(8,128)S(1)} %get-tuple-element.65), channel_id=1, source_target_pairs={{0,4},{4,0},{1,5},{5,1},{2,6},{6,2},{3,7},{7,3},{8,12},{12,8},{9,1... | collective-permute-start | bytes 847880 | tf_op jit(solution)/shard_map/ppermute | solution.py:458
  1.4 24.9 %collective-permute-start.5 = (f32[552,128]{1,0:T(8,128)S(1)}, f32[552,128]{1,0:T(8,128)S(1)}, u32[]{:S(2)}, u32[]{:S(2)}) collective-permute-start(f32[552,128]{1,0:T(8,128)S(1)} %get-tuple-element.66), channel_id=1, source_target_pairs={{4,8},{8,4},{5,9},{9,5},{6,10},{10,6},{7,11},{11,7},{20,24},{24,20... | collective-permute-start | bytes 847880 | tf_op jit(solution)/shard_map/ppermute | solution.py:459
  10.0 21.9 %collective-permute-start = (f32[512,128]{1,0:T(8,128)S(1)}, f32[512,128]{1,0:T(8,128)S(1)}, u32[]{:S(2)}, u32[]{:S(2)}) collective-permute-start(f32[512,128]{1,0:T(8,128)S(1)} %get-tuple-element.56), channel_id=1, source_target_pairs={{4,8},{8,4},{5,9},{9,5},{6,10},{10,6},{7,11},{11,7},{20,24},{24,20... | collective-permute-start | bytes 786440 | tf_op jit(solution)/shard_map/ppermute | solution.py:459
  11.9 20.0 %collective-permute-start.1 = (f32[512,128]{1,0:T(8,128)S(1)}, f32[512,128]{1,0:T(8,128)S(1)}, u32[]{:S(2)}, u32[]{:S(2)}) collective-permute-start(f32[512,128]{1,0:T(8,128)S(1)} %get-tuple-element.57), channel_id=1, source_target_pairs={{0,4},{4,0},{1,5},{5,1},{2,6},{6,2},{3,7},{7,3},{8,12},{12,8},{9,1... | collective-permute-start | bytes 786440 | tf_op jit(solution)/shard_map/ppermute | solution.py:458
  15.5 10.7 %copy-start = (f32[1,16,16,128]{3,2,1,0:T(8,128)S(1)}, f32[1,16,16,128]{3,2,1,0:T(8,128)}, u32[]{:S(2)}) copy-start(f32[1,16,16,128]{3,2,1,0:T(8,128)} %param.5) | copy-start | bytes 393220
  26.4 9.6 %collective-permute-start.6 = (f32[608,128]{1,0:T(8,128)S(1)}, f32[608,128]{1,0:T(8,128)S(1)}, u32[]{:S(2)}, u32[]{:S(2)}) collective-permute-start(f32[608,128]{1,0:T(8,128)S(1)} %get-tuple-element.70), channel_id=1, source_target_pairs={{1,2},{2,1},{5,6},{6,5},{9,10},{10,9},{13,14},{14,13},{17,18},{18,... | collective-permute-start | bytes 933896 | tf_op jit(solution)/shard_map/ppermute | solution.py:459
  28.3 7.7 %collective-permute-start.7 = (f32[608,128]{1,0:T(8,128)S(1)}, f32[608,128]{1,0:T(8,128)S(1)}, u32[]{:S(2)}, u32[]{:S(2)}) collective-permute-start(f32[608,128]{1,0:T(8,128)S(1)} %get-tuple-element.71), channel_id=1, source_target_pairs={{0,1},{1,0},{2,3},{3,2},{4,5},{5,4},{6,7},{7,6},{8,9},{9,8},{10,11... | collective-permute-start | bytes 933896 | tf_op jit(solution)/shard_map/ppermute | solution.py:458
  32.0 10.9 %collective-permute-start.2 = (f32[544,128]{1,0:T(8,128)S(1)}, f32[544,128]{1,0:T(8,128)S(1)}, u32[]{:S(2)}, u32[]{:S(2)}) collective-permute-start(f32[544,128]{1,0:T(8,128)S(1)} %get-tuple-element.59), channel_id=1, source_target_pairs={{1,2},{2,1},{5,6},{6,5},{9,10},{10,9},{13,14},{14,13},{17,18},{18,... | collective-permute-start | bytes 835592 | tf_op jit(solution)/shard_map/ppermute | solution.py:459
  35.9 7.0 %collective-permute-start.3 = (f32[544,128]{1,0:T(8,128)S(1)}, f32[544,128]{1,0:T(8,128)S(1)}, u32[]{:S(2)}, u32[]{:S(2)}) collective-permute-start(f32[544,128]{1,0:T(8,128)S(1)} %get-tuple-element.60), channel_id=1, source_target_pairs={{0,1},{1,0},{2,3},{3,2},{4,5},{5,4},{6,7},{7,6},{8,9},{9,8},{10,11... | collective-permute-start | bytes 835592 | tf_op jit(solution)/shard_map/ppermute | solution.py:458
  37.7 13.4 %collective-permute-start.10 = (f32[512,128]{1,0:T(8,128)S(1)}, f32[512,128]{1,0:T(8,128)S(1)}, u32[]{:S(2)}, u32[]{:S(2)}) collective-permute-start(f32[512,128]{1,0:T(8,128)S(1)} %get-tuple-element.80), channel_id=1, source_target_pairs={{0,4},{4,0},{1,5},{5,1},{2,6},{6,2},{3,7},{7,3},{8,12},{12,8},{9,1... | collective-permute-start | bytes 786440 | tf_op jit(solution)/shard_map/ppermute | solution.py:458
  37.8 23.4 %collective-permute-start.11 = (f32[512,128]{1,0:T(8,128)S(1)}, f32[512,128]{1,0:T(8,128)S(1)}, u32[]{:S(2)}, u32[]{:S(2)}) collective-permute-start(f32[512,128]{1,0:T(8,128)S(1)} %get-tuple-element.81), channel_id=1, source_target_pairs={{4,8},{8,4},{5,9},{9,5},{6,10},{10,6},{7,11},{11,7},{20,24},{24,20... | collective-permute-start | bytes 786440 | tf_op jit(solution)/shard_map/ppermute | solution.py:459
  44.6 22.2 %collective-permute-start.8 = (f32[512,128]{1,0:T(8,128)S(1)}, f32[512,128]{1,0:T(8,128)S(1)}, u32[]{:S(2)}, u32[]{:S(2)}) collective-permute-start(f32[512,128]{1,0:T(8,128)S(1)} %get-tuple-element.77), channel_id=1, source_target_pairs={{4,8},{8,4},{5,9},{9,5},{6,10},{10,6},{7,11},{11,7},{20,24},{24,20... | collective-permute-start | bytes 786440 | tf_op jit(solution)/shard_map/ppermute | solution.py:459
  47.2 19.6 %collective-permute-start.9 = (f32[512,128]{1,0:T(8,128)S(1)}, f32[512,128]{1,0:T(8,128)S(1)}, u32[]{:S(2)}, u32[]{:S(2)}) collective-permute-start(f32[512,128]{1,0:T(8,128)S(1)} %get-tuple-element.78), channel_id=1, source_target_pairs={{0,4},{4,0},{1,5},{5,1},{2,6},{6,2},{3,7},{7,3},{8,12},{12,8},{9,1... | collective-permute-start | bytes 786440 | tf_op jit(solution)/shard_map/ppermute | solution.py:458
  61.4 9.2 %collective-permute-start.14 = (f32[704,128]{1,0:T(8,128)S(1)}, f32[704,128]{1,0:T(8,128)S(1)}, u32[]{:S(2)}, u32[]{:S(2)}) collective-permute-start(f32[704,128]{1,0:T(8,128)S(1)} %get-tuple-element.98), channel_id=1, source_target_pairs={{1,2},{2,1},{5,6},{6,5},{9,10},{10,9},{13,14},{14,13},{17,18},{18,... | collective-permute-start | bytes 1081352 | tf_op jit(solution)/shard_map/ppermute | solution.py:459
  63.3 7.3 %collective-permute-start.15 = (f32[704,128]{1,0:T(8,128)S(1)}, f32[704,128]{1,0:T(8,128)S(1)}, u32[]{:S(2)}, u32[]{:S(2)}) collective-permute-start(f32[704,128]{1,0:T(8,128)S(1)} %get-tuple-element.99), channel_id=1, source_target_pairs={{0,1},{1,0},{2,3},{3,2},{4,5},{5,4},{6,7},{7,6},{8,9},{9,8},{10,11... | collective-permute-start | bytes 1081352 | tf_op jit(solution)/shard_map/ppermute | solution.py:458
  67.0 8.7 %collective-permute-start.12 = (f32[704,128]{1,0:T(8,128)S(1)}, f32[704,128]{1,0:T(8,128)S(1)}, u32[]{:S(2)}, u32[]{:S(2)}) collective-permute-start(f32[704,128]{1,0:T(8,128)S(1)} %get-tuple-element.95), channel_id=1, source_target_pairs={{1,2},{2,1},{5,6},{6,5},{9,10},{10,9},{13,14},{14,13},{17,18},{18,... | collective-permute-start | bytes 1081352 | tf_op jit(solution)/shard_map/ppermute | solution.py:459
  68.9 6.8 %collective-permute-start.13 = (f32[704,128]{1,0:T(8,128)S(1)}, f32[704,128]{1,0:T(8,128)S(1)}, u32[]{:S(2)}, u32[]{:S(2)}) collective-permute-start(f32[704,128]{1,0:T(8,128)S(1)} %get-tuple-element.96), channel_id=1, source_target_pairs={{0,1},{1,0},{2,3},{3,2},{4,5},{5,4},{6,7},{7,6},{8,9},{9,8},{10,11... | collective-permute-start | bytes 1081352 | tf_op jit(solution)/shard_map/ppermute | solution.py:458
